TPU v7x, 512 devices: a whole 4x8x8 slice. The times are simulated.
512 devices in a mesh: dp: 32 (over z, y_lo), ctx: 16 (over x, y_hi, core).
Axes of the slice: x: 4, y: 8 (y_hi: 2, y_lo: 4; y = y_hi * 4 + y_lo), z: 8, core: 2. Of those that a mesh axis runs over, the one named last changes fastest.
Arguments:
- frame_input: bfloat16 [64, 1024, 1536], P('dp', 'ctx'), may hold values from -6 to 6
- queries: bfloat16 [64, 1024, 768], P('dp', 'ctx'), may hold values from -18 to 18
- key_proj: bfloat16 [64, 1024, 768], P('dp', 'ctx'), may hold values from -18 to 18
- value_proj: bfloat16 [64, 1024, 768], P('dp', 'ctx'), may hold values from -6 to 6
- out_weight: bfloat16 [1536, 768], P('ctx', 'dp'), may hold values from -0.21875 to 0.21875
- conv_weight: bfloat16 [31, 1536], P(None, 'dp'), may hold values from -1 to 1
- lengths: int32 [64], P('dp'), may hold values from 256 to 1024, as said below
- grad_output: bfloat16 [64, 1024, 1536], P('dp', 'ctx'), may hold values from -6 to 6
Outputs:
- block_output: bfloat16 [64, 1024, 1536], P('dp', 'ctx')
- grad_input: bfloat16 [64, 1024, 1536], P('dp', 'ctx')
- grad_queries: bfloat16 [64, 1024, 768], P('dp', 'ctx')
- grad_keys: bfloat16 [64, 1024, 768], P('dp', 'ctx')
- grad_values: bfloat16 [64, 1024, 768], P('dp', 'ctx')
- grad_out_weight: float32 [1536, 768], P('ctx', 'dp')
- grad_conv_weight: float32 [31, 1536], P(None, 'dp')
Inputs may be any that keep to these rules, and one draw needn't show every extreme that they name: `lengths`: at least one utterance of every draw fills all 1024 frame slots.
All inputs are finite; a program needn't handle non-finite values.
Results may differ from a plain program's by a relative error of at most 0.035.
Values may be sent and summed in bfloat16 or wider, within the bound.
A program may use at most 128 MiB of HBM per device.

v0:
```python
import jax
import jax.numpy as jnp
from jax import lax
from jax.sharding import PartitionSpec as P

HEAD_DIM = 64


masked_score = -1e30


def padded_2(array, sides, width):
    for axis, dim in sides:
        size, length = (lax.axis_size(axis), array.shape[dim])
        up = [(i, (i + 1) % size) for i in range(size - 1)]
        down = [(j, i) for i, j in up]
        last = lax.slice_in_dim(array, length - width, length, axis=dim)
        leading = lax.slice_in_dim(array, 0, width, axis=dim)
        before = lax.ppermute(last, axis, up)
        after = lax.ppermute(leading, axis, down)
        array = jnp.concatenate([before, array, after], axis=dim)
    return array


def depthwise(lhs, rhs):
    return lax.conv_general_dilated(
        lhs,
        rhs,
        (1,),
        "VALID",
        dimension_numbers=("NWC", "WIO", "NWC"),
        feature_group_count=lhs.shape[2],
        precision=lax.Precision.HIGHEST,
    )


def per_device(
    frame_input, queries, key_proj, value_proj, out_weight, conv_weight, lengths, grad_output
):
    utt_count = frame_input.shape[0]
    frame_count = frame_input.shape[1]
    inner_width = queries.shape[2]
    head_count = inner_width // HEAD_DIM
    group_heads = max((g for g in range(1, 7) if head_count % g == 0))
    group_count = head_count // group_heads
    group_width = group_heads * HEAD_DIM
    tap_count = conv_weight.shape[0]
    half_span = (tap_count - 1) // 2
    score_scale = HEAD_DIM ** (-0.5)
    total_frames = frame_count * lax.axis_size("ctx")
    offset = lax.axis_index("ctx") * frame_count
    own_valid = (offset + jnp.arange(frame_count, dtype=jnp.int32))[None, :] < lengths[:, None]
    all_valid = jnp.arange(total_frames, dtype=jnp.int32)[None, :] < lengths[:, None]

    def grouped(values):
        row_count = values.shape[1]
        return values.reshape(utt_count, row_count, group_count, group_width).transpose(2, 0, 1, 3)

    def ungrouped(values):
        row_count = values.shape[2]
        return values.transpose(1, 2, 0, 3).reshape(utt_count, row_count, group_count * group_width)

    def split_heads(values):
        return values.reshape(utt_count, values.shape[1], group_heads, HEAD_DIM)

    def stats_grouped(values):
        row_count = values.shape[1]
        return values.reshape(utt_count, row_count, group_count, group_heads).transpose(2, 0, 3, 1)

    def masked_scores(query_block, key_block, key_mask):
        scores = (
            jnp.einsum(
                "uqgd,ukgd->ugqk", query_block, key_block, preferred_element_type=jnp.float32
            )
            * score_scale
        )
        return jnp.where(key_mask[:, None, None, :], scores, masked_score)

    taps = lax.all_gather(conv_weight, "dp", axis=1, tiled=True).astype(jnp.float32)
    panel_rows = lax.all_gather(out_weight, "dp", axis=1, tiled=True)
    weight_full = lax.all_gather(panel_rows, "ctx", axis=0, tiled=True)
    all_keys, all_values = (
        lax.all_gather(key_proj, "ctx", axis=1, tiled=True),
        lax.all_gather(value_proj, "ctx", axis=1, tiled=True),
    )
    query_groups = grouped(queries)
    key_groups = grouped(all_keys)
    value_groups = grouped(all_values)

    def forward_group(unused, items):
        query_group, key_group, value_group = items
        query_block = split_heads(query_group)
        scores = masked_scores(query_block, split_heads(key_group), all_valid)
        largest = jnp.max(scores, axis=-1)
        log_group = largest + jnp.log(jnp.sum(jnp.exp(scores - largest[..., None]), axis=-1))
        weights_low = jnp.exp(scores - log_group[..., None]).astype(jnp.bfloat16)
        attended_group = jnp.einsum(
            "ugqk,ukgd->uqgd",
            weights_low,
            split_heads(value_group),
            preferred_element_type=jnp.float32,
        )
        return (None, (log_group, attended_group.reshape(utt_count, frame_count, group_width)))

    _, (log_groups, attended_groups) = lax.scan(
        forward_group, None, (query_groups, key_groups, value_groups)
    )
    attended = ungrouped(attended_groups).astype(jnp.bfloat16)
    log_total = log_groups.transpose(1, 3, 0, 2).reshape(utt_count, frame_count, head_count)
    projected = jnp.einsum("ufe,de->ufd", attended, weight_full, preferred_element_type=jnp.float32)
    hidden = (frame_input.astype(jnp.float32) + projected).astype(jnp.bfloat16)
    masked_hidden = jnp.where(own_valid[:, :, None], hidden, jnp.zeros_like(hidden))
    padded = padded_2(masked_hidden, (("ctx", 1),), half_span).astype(jnp.float32)
    conv_sum = depthwise(padded, taps[:, None, :])
    sigmoid = jax.nn.sigmoid(conv_sum)
    block_output = (hidden.astype(jnp.float32) + conv_sum * sigmoid).astype(jnp.bfloat16)
    grad_local = grad_output.astype(jnp.float32)
    swish_slope = sigmoid * (1.0 + conv_sum * (1.0 - sigmoid))
    grad_conv = (grad_local * swish_slope).astype(jnp.bfloat16)
    grad_padded = padded_2(grad_conv, (("ctx", 1),), half_span).astype(jnp.float32)
    back_sum = depthwise(grad_padded, taps[::-1][:, None, :])
    grad_hidden = (grad_local + jnp.where(own_valid[:, :, None], back_sum, 0.0)).astype(
        jnp.bfloat16
    )
    grad_conv_wide = grad_conv.astype(jnp.float32)
    kernel_term = jnp.zeros((tap_count, conv_sum.shape[2]), jnp.float32)
    for utt_index in range(utt_count):
        kernel_term = (
            kernel_term
            + depthwise(padded[utt_index : utt_index + 1], grad_conv_wide[utt_index][:, None, :])[0]
        )
    kernel_whole = lax.psum(kernel_term.astype(jnp.bfloat16), "ctx")
    grad_conv_weight = lax.psum_scatter(kernel_whole, "dp", scatter_dimension=1, tiled=True).astype(
        jnp.float32
    )
    grad_attended = jnp.einsum(
        "ufd,de->ufe", grad_hidden, weight_full, preferred_element_type=jnp.float32
    ).astype(jnp.bfloat16)
    row_delta = jnp.sum(
        grad_attended.astype(jnp.float32).reshape(utt_count, frame_count, head_count, HEAD_DIM)
        * attended.astype(jnp.float32).reshape(utt_count, frame_count, head_count, HEAD_DIM),
        axis=-1,
    )
    grad_groups = grouped(grad_attended)

    def query_group_step(unused, items):
        query_group, key_group, value_group, grad_group, log_group, delta_group = items
        key_block = split_heads(key_group)
        weights = jnp.exp(
            masked_scores(split_heads(query_group), key_block, all_valid) - log_group[..., None]
        )
        grad_weights = jnp.einsum(
            "uqgd,ukgd->ugqk",
            split_heads(grad_group),
            split_heads(value_group),
            preferred_element_type=jnp.float32,
        )
        grad_scores = (weights * (grad_weights - delta_group[..., None])).astype(jnp.bfloat16)
        query_sum = jnp.einsum(
            "ugqk,ukgd->uqgd", grad_scores, key_block, preferred_element_type=jnp.float32
        )
        return (None, query_sum.reshape(utt_count, frame_count, group_width))

    _, query_sums = lax.scan(
        query_group_step,
        None,
        (
            query_groups,
            key_groups,
            value_groups,
            grad_groups,
            stats_grouped(log_total),
            stats_grouped(row_delta),
        ),
    )
    grad_queries = (ungrouped(query_sums) * score_scale).astype(jnp.bfloat16)
    total_log, total_delta = (
        lax.all_gather(log_total, "ctx", axis=1, tiled=True),
        lax.all_gather(row_delta, "ctx", axis=1, tiled=True),
    )
    own_key_groups = grouped(key_proj)
    own_value_groups = grouped(value_proj)
    group_zeros = jnp.zeros((group_count, utt_count, frame_count, group_width), jnp.float32)
    start_sums = (group_zeros, group_zeros)
    query_all, grad_all = (
        lax.all_gather(queries, "ctx", axis=1, tiled=True),
        lax.all_gather(grad_attended, "ctx", axis=1, tiled=True),
    )
    log_piece = stats_grouped(total_log)
    delta_piece = stats_grouped(total_delta)

    def key_group_step(unused, items):
        (
            query_group,
            grad_group,
            log_group,
            delta_group,
            key_group,
            value_group,
            key_sum,
            value_sum,
        ) = items
        query_block = split_heads(query_group)
        grad_block = split_heads(grad_group)
        weights = jnp.exp(
            masked_scores(query_block, split_heads(key_group), own_valid) - log_group[..., None]
        )
        grad_weights = jnp.einsum(
            "uqgd,ukgd->ugqk",
            grad_block,
            split_heads(value_group),
            preferred_element_type=jnp.float32,
        )
        grad_scores = (weights * (grad_weights - delta_group[..., None])).astype(jnp.bfloat16)
        key_next = key_sum + jnp.einsum(
            "ugqk,uqgd->ukgd", grad_scores, query_block, preferred_element_type=jnp.float32
        ).reshape(utt_count, frame_count, group_width)
        value_next = value_sum + jnp.einsum(
            "ugqk,uqgd->ukgd",
            weights.astype(jnp.bfloat16),
            grad_block,
            preferred_element_type=jnp.float32,
        ).reshape(utt_count, frame_count, group_width)
        return (None, (key_next, value_next))

    _, result_sums = lax.scan(
        key_group_step,
        None,
        (
            grouped(query_all),
            grouped(grad_all),
            log_piece,
            delta_piece,
            own_key_groups,
            own_value_groups,
            start_sums[0],
            start_sums[1],
        ),
    )
    key_sum, value_sum = result_sums
    grad_keys = (ungrouped(key_sum) * score_scale).astype(jnp.bfloat16)
    grad_values = ungrouped(value_sum).astype(jnp.bfloat16)
    hidden_cols = lax.slice_in_dim(
        grad_hidden, 0, weight_full.shape[0] // lax.axis_size("ctx") * lax.axis_size("ctx"), axis=2
    )
    panel_share = lax.psum_scatter(
        jnp.einsum("ufd,ufe->de", hidden_cols, attended, preferred_element_type=jnp.float32).astype(
            jnp.bfloat16
        ),
        "ctx",
        scatter_dimension=0,
        tiled=True,
    )
    grad_out_weight = lax.psum_scatter(panel_share, "dp", scatter_dimension=1, tiled=True).astype(
        jnp.float32
    )
    return (
        block_output,
        grad_hidden,
        grad_queries,
        grad_keys,
        grad_values,
        grad_out_weight,
        grad_conv_weight,
    )


def solution(mesh):
    placed = (
        P("dp", "ctx", None),
        P("dp", "ctx", None),
        P("dp", "ctx", None),
        P("dp", "ctx", None),
        P("ctx", "dp"),
        P(None, "dp"),
        P("dp"),
        P("dp", "ctx", None),
    )
    return jax.shard_map(
        per_device,
        mesh=mesh,
        in_specs=placed,
        out_specs=(
            P("dp", "ctx", None),
            P("dp", "ctx", None),
            P("dp", "ctx", None),
            P("dp", "ctx", None),
            P("dp", "ctx", None),
            P("ctx", "dp"),
            P(None, "dp"),
        ),
        check_vma=False,
    )
```

profile of v0, /device:TPU:1, one launch (start us, length us, event | category | flops | bytes accessed | tf_op | source)
XLA Modules:
  0.0 1105.4 jit_solution(739384458572072141)
XLA Ops:
  9.1 1.8 copy.133
  11.0 77.3 %all_gather.29 = bf16[96,768]{0,1:T(8,128)(2,1)S(1)} all-gather(bf16[96,24]{0,1:T(8,128)(2,1)} %param.18), channel_id=1, replica_groups=mesh['dp'=32,'ctx'=16] {'dp'}, dimensions={1}, use_global_device_ids=true | all-gather | bytes 152064 | tf_op jit(solution)/shard_map/all_gather | solution.py:80
  92.1 2.1 all-gather.7.cloned.1.call-done
  94.3 7.0 copy.132
  101.3 2.0 copy.136
  103.3 64.5 %all-gather.9.cloned.1.call-done = bf16[2,1024,768]{2,0,1:T(2,128)(2,1)} async-done(((bf16[2,64,768]{2,0,1:T(2,128)(2,1)}), bf16[2,1024,768]{2,0,1:T(2,128)(2,1)}) %all-gather.9.cloned.1.call-update) | async-done | bytes 3145744 | tf_op jit(solution)/shard_map/all_gather | solution.py:84
  167.8 7.0 copy.134
  174.8 2.0 copy.137
  176.9 16.0 %while.37 = (s32[]{:T(128)}, f32[2,2,6,64]{3,2,1,0:T(8,128)}, bf16[2,2,64,384]{3,2,0,1:T(8,128)(2,1)}, bf16[2,2,64,384]{3,2,1,0:T(8,128)(2,1)}, bf16[2,2,1024,38...) while((s32[]{:T(128)}, f32[2,2,6,64]{3,2,1,0:T(8,128)}, ...), condition=%wide.region_3.4_spmd.clone, body=%wide.region_0.3_spmd.clone.sunk | while | flops 209978624 | bytes 21468332 | solution.py:105
  177.6 2.2 constant_dynamic-slice_fusion.23
  185.6 2.2 constant_dynamic-slice_fusion.23
  193.8 43.9 %all-gather.11.cloned.1.call-done = bf16[1536,768]{1,0:T(8,128)(2,1)} async-done(((bf16[96,768]{1,0:T(8,128)(2,1)}), bf16[1536,768]{1,0:T(8,128)(2,1)}) %all-gather.11.cloned.1.call-update) | async-done | bytes 2359312 | tf_op jit(solution)/shard_map/all_gather | solution.py:81
  237.7 2.6 broadcast_select_fusion
  240.3 2.2 collective-permute-start.1
  242.5 7.3 collective-permute-start
  249.8 64.3 %all-gather = bf16[32,48,31]{1,2,0:T(8,128)(2,1)S(1)} all-gather(bf16[1,48,31]{1,2,0:T(8,128)(2,1)S(1)} %bitcast.212), channel_id=1, replica_groups=mesh['dp'=32,'ctx'=16] {'dp'}, dimensions={0}, use_global_device_ids=true | all-gather | bytes 98208 | tf_op jit(solution)/shard_map/all_gather | solution.py:79
  314.8 2.7 fusion.54
  318.6 11.0 collective-permute-start.3
  329.6 6.8 collective-permute-start.2
  338.3 2.3 fusion.52
  340.9 2.2 bitcast_convert_fusion
  344.2 1.9 fusion.49
  346.1 1.9 fusion.43
  349.2 90.0 %reduce-scatter.6.cloned.1.call-done = bf16[96,768]{1,0:T(8,128)(2,1)} async-done(((bf16[1536,768]{1,0:T(8,128)(2,1)}), bf16[96,768]{1,0:T(8,128)(2,1)}) %reduce-scatter.6.cloned.1.call-update) | async-done | bytes 147472 | tf_op jit(solution)/shard_map/reduce_scatter | solution.py:246
  446.6 42.3 %all_gather.33 = f32[2,1024,12]{2,0,1:T(2,128)S(1)} all-gather(f32[2,64,12]{2,0,1:T(2,128)S(1)} %copy.161), channel_id=1, replica_groups=mesh['dp'=32,'ctx'=16] {'ctx'}, dimensions={1}, use_global_device_ids=true | all-gather | bytes 104448 | tf_op jit(solution)/shard_map/all_gather | solution.py:178
  490.0 29.2 %all-gather.13.cloned.1.call-done = bf16[2,1024,768]{2,0,1:T(2,128)(2,1)} async-done(((bf16[2,64,768]{2,0,1:T(2,128)(2,1)}), bf16[2,1024,768]{2,0,1:T(2,128)(2,1)}) %all-gather.13.cloned.1.call-update) | async-done | bytes 3145744 | tf_op jit(solution)/shard_map/all_gather | solution.py:186
  519.1 8.7 copy.159
  531.5 29.7 %while.38 = (s32[]{:T(128)}, f32[2,2,64,384]{2,3,1,0:T(8,128)}, bf16[2,2,1024,384]{2,3,1,0:T(8,128)(2,1)}, bf16[2,2,64,384]{3,2,1,0:T(8,128)(2,1)}, f32[2,2,6,64...) while((s32[]{:T(128)}, f32[2,2,64,384]{2,3,1,0:T(8,128)}, ...), condition=%wide.region_6.7_spmd.clone, body=%wide.region_5.6_spmd.clone.sunk | while | flops 306710528 | bytes 19099784 | solution.py:164
  531.5 2.2 constant_dynamic-slice_fusion.25
  536.4 2.2 fusion.108
  542.2 3.4 fusion.109
  546.3 2.2 constant_dynamic-slice_fusion.25
  551.2 2.2 fusion.108
  557.0 3.4 fusion.109
  563.4 37.6 %all_gather.35 = f32[2,1024,12]{2,0,1:T(2,128)S(1)} all-gather(f32[2,64,12]{2,0,1:T(2,128)} %copy.164), channel_id=1, replica_groups=mesh['dp'=32,'ctx'=16] {'ctx'}, dimensions={1}, use_global_device_ids=true | all-gather | bytes 104448 | tf_op jit(solution)/shard_map/all_gather | solution.py:179
  601.5 59.2 %reduce-scatter.8.cloned.1.call-done = bf16[48,31]{1,0:T(8,128)(2,1)} async-done(((bf16[1536,31]{1,0:T(8,128)(2,1)}), bf16[48,31]{1,0:T(8,128)(2,1)}) %reduce-scatter.8.cloned.1.call-update) | async-done | bytes 2992
  661.6 68.0 %psum.8 = bf16[31,48]{1,0:T(8,128)(2,1)S(1)} all-reduce(bf16[31,48]{1,0:T(8,128)(2,1)S(1)} %copy.181), channel_id=1, replica_groups=mesh['dp'=32,'ctx'=16] {'ctx'}, use_global_device_ids=true, to_apply=%region_11.12 | all-reduce | flops 1488 | bytes 5952 | tf_op jit(solution)/shard_map/psum | solution.py:132
  730.2 222.8 %all-reduce.3.cloned.1.call-done = bf16[96,768]{1,0:T(8,128)(2,1)} async-done(((bf16[96,768]{1,0:T(8,128)(2,1)}), bf16[96,768]{1,0:T(8,128)(2,1)}) %all-reduce.3.cloned.1.call-update) | async-done | bytes 147472
  954.5 91.6 %all-gather.15.cloned.1.call-done = bf16[2,1024,768]{2,1,0:T(8,128)(2,1)} async-done(((bf16[2,64,768]{2,1,0:T(8,128)(2,1)}), bf16[2,1024,768]{2,1,0:T(8,128)(2,1)}) %all-gather.15.cloned.1.call-update) | async-done | bytes 3145744 | tf_op jit(solution)/shard_map/all_gather | solution.py:187
  1046.1 5.8 reshape.203
  1051.9 6.9 copy.163
  1059.8 34.6 %while.39 = (s32[]{:T(128)}, f32[2,2,64,384]{2,3,1,0:T(8,128)}, bf16[2,2,64,384]{2,3,1,0:T(8,128)(2,1)}, bf16[2,2,1024,384]{2,3,0,1:T(8,128)(2,1)}, bf16[2,2,64,...) while((s32[]{:T(128)}, f32[2,2,64,384]{2,3,1,0:T(8,128)}, ...), condition=%wide.region_8.9_spmd.clone, body=%wide.region_7.8_spmd.clone.sunk | while | flops 410517632 | bytes 39764904 | solution.py:226
  1062.5 2.3 fusion.117
  1069.1 3.3 fusion.118
  1073.2 3.0 fusion.119
  1079.8 2.3 fusion.117
  1086.4 3.3 fusion.118
  1090.5 3.0 fusion.119
  (180 shorter events, 77.7 us)
Async XLA Ops:
  7.2 87.1 %all-gather.7.cloned.1.call-start = ((), (), s32[]{:S(2)}) async-start(), calls=%async_computation.2 | async-start | bytes 3342336 | tf_op jit(solution)/shard_map/all_gather | solution.py:83
  9.0 158.8 %all-gather.9.cloned.1.call-start = ((), (), s32[]{:S(2)}) async-start(), calls=%async_computation.3 | async-start | bytes 3342336 | tf_op jit(solution)/shard_map/all_gather | solution.py:84
  10.9 226.8 %all-gather.11.cloned.1.call-start = ((), (), s32[]{:S(2)}) async-start(), calls=%async_computation.4 | async-start | bytes 2506752 | tf_op jit(solution)/shard_map/all_gather | solution.py:81
  89.1 350.1 %reduce-scatter.6.cloned.1.call-start = ((), (), s32[]{:S(2)}) async-start(), calls=%async_computation.7 | async-start | bytes 2506752 | tf_op jit(solution)/shard_map/reduce_scatter | solution.py:246
  90.8 0.6 copy-start.16
  182.9 1.2 copy-start.12
  184.2 0.7 copy-start.13
  190.9 1.2 copy-start.12
  192.2 0.7 copy-start.13
  192.9 57.0 %copy-start.15 = (bf16[31,48]{1,0:T(8,128)(2,1)S(1)}, bf16[31,48]{1,0:T(8,128)(2,1)}, u32[]{:S(2)}) copy-start(bf16[31,48]{1,0:T(8,128)(2,1)} %param.19) | copy-start | bytes 8932
  240.3 74.3 %collective-permute-start.1 = (bf16[2,15,1536]{2,1,0:T(8,128)(2,1)S(1)}, bf16[2,15,1536]{2,1,0:T(8,128)(2,1)S(1)}, u32[]{:S(2)}, u32[]{:S(2)}) collective-permute-start(bf16[2,15,1536]{2,1,0:T(8,128)(2,1)S(1)} %get-tuple-element.409), channel_id=1, source_target_pairs={{1,0},{2,1},{3,2},{4,3},{5,4},{6,5},{7,6},{8,7},{9,8},{10,9},{11,1... | collective-permute-start | bytes 276488 | tf_op jit(solution)/shard_map/ppermute | solution.py:20
  242.5 72.1 %collective-permute-start = (bf16[2,15,1536]{2,1,0:T(8,128)(2,1)S(1)}, bf16[2,15,1536]{2,1,0:T(8,128)(2,1)S(1)}, u32[]{:S(2)}, u32[]{:S(2)}) collective-permute-start(bf16[2,15,1536]{2,1,0:T(8,128)(2,1)S(1)} %get-tuple-element.408), channel_id=1, source_target_pairs={{0,1},{1,2},{2,3},{3,4},{4,5},{5,6},{6,7},{7,8},{8,9},{9,10},{10,1... | collective-permute-start | bytes 276488 | tf_op jit(solution)/shard_map/ppermute | solution.py:19
  314.8 2.7 copy-start.4
  318.6 18.2 %collective-permute-start.3 = (bf16[2,15,1536]{2,1,0:T(8,128)(2,1)S(1)}, bf16[2,15,1536]{2,1,0:T(8,128)(2,1)S(1)}, u32[]{:S(2)}, u32[]{:S(2)}) collective-permute-start(bf16[2,15,1536]{2,1,0:T(8,128)(2,1)S(1)} %get-tuple-element.407), channel_id=1, source_target_pairs={{1,0},{2,1},{3,2},{4,3},{5,4},{6,5},{7,6},{8,7},{9,8},{10,9},{11,1... | collective-permute-start | bytes 276488 | tf_op jit(solution)/shard_map/ppermute | solution.py:20
  329.6 8.5 collective-permute-start.2
  340.6 2.6 copy-start.9
  340.9 98.6 %copy-start.2 = (bf16[2,64,1536]{2,1,0:T(8,128)(2,1)}, bf16[2,64,1536]{2,1,0:T(8,128)(2,1)S(1)}, u32[]{:S(2)}) copy-start(bf16[2,64,1536]{2,1,0:T(8,128)(2,1)S(1)} %fusion.48) | copy-start | bytes 1179652
  343.1 176.0 %all-gather.13.cloned.1.call-start = ((), (), s32[]{:S(2)}) async-start(), calls=%async_computation.5 | async-start | bytes 3342336 | tf_op jit(solution)/shard_map/all_gather | solution.py:186
  344.1 316.7 %reduce-scatter.8.cloned.1.call-start = ((), (), s32[]{:S(2)}) async-start(), calls=%async_computation.8 | async-start | bytes 405504
  346.1 93.4 %copy-start.1 = (bf16[1536,768]{1,0:T(8,128)(2,1)S(1)}, bf16[1536,768]{1,0:T(8,128)(2,1)}, u32[]{:S(2)}) copy-start(bf16[1536,768]{1,0:T(8,128)(2,1)} %all-gather.11.cloned.1.call-done) | copy-start | bytes 7077892
  348.1 92.6 %copy-start.10 = (bf16[2,64,768]{2,1,0:T(8,128)(2,1)S(1)}, bf16[2,64,768]{2,1,0:T(8,128)(2,1)}, u32[]{:S(2)}) copy-start(bf16[2,64,768]{2,1,0:T(8,128)(2,1)} %param.16) | copy-start | bytes 589828
  348.1 92.6 %copy-start.11 = (bf16[2,64,768]{2,1,0:T(8,128)(2,1)S(1)}, bf16[2,64,768]{2,1,0:T(8,128)(2,1)}, u32[]{:S(2)}) copy-start(bf16[2,64,768]{2,1,0:T(8,128)(2,1)} %param.17) | copy-start | bytes 589828
  348.1 96.8 %copy-start.14 = (bf16[2,2,64,384]{3,2,0,1:T(8,128)(2,1)S(1)}, bf16[2,2,64,384]{3,2,0,1:T(8,128)(2,1)}, u32[]{:S(2)}) copy-start(bf16[2,2,64,384]{3,2,0,1:T(8,128)(2,1)} %get-tuple-element.145) | copy-start | bytes 589828
  349.1 603.8 %all-reduce.3.cloned.1.call-start = ((), (), s32[]{:S(2)}) async-start(), calls=%async_computation.9 | async-start | bytes 294912
  439.2 606.9 %all-gather.15.cloned.1.call-start = ((), (), s32[]{:S(2)}) async-start(), calls=%async_computation.6 | async-start | bytes 3342336 | tf_op jit(solution)/shard_map/all_gather | solution.py:187
  490.0 37.9 %copy-start.3 = (bf16[2,64,768]{2,1,0:T(8,128)(2,1)S(1)}, bf16[2,64,768]{2,1,0:T(8,128)(2,1)}, u32[]{:S(2)}) copy-start(bf16[2,64,768]{2,1,0:T(8,128)(2,1)} %fusion.44) | copy-start | bytes 589828
  1051.9 7.8 copy-start.17
  1059.8 5.6 copy-start.7
  1062.5 2.8 copy-start
  1073.2 3.0 copy-start.5
  1073.2 3.8 copy-start.8
  1076.3 0.7 copy-start.6
  1077.1 5.6 copy-start.7
  1079.8 2.8 copy-start
  1090.5 3.0 copy-start.5
  1090.5 3.8 copy-start.8
  1093.6 0.7 copy-start.6
Sparse Core Ops, SparseCore 0:
  11.8 82.3 all-gather.6
  98.1 69.6 all-gather.8
  171.7 65.9 all-gather.10
  343.3 95.8 reduce-scatter.5
  442.9 76.1 all-gather.12
  521.8 138.9 reduce-scatter.7
  663.9 288.9 all-reduce.2
  956.3 89.7 all-gather.14
where the time goes:
time: 1110 us
  waiting for transfers between devices  605 us (55%)
  blocking collectives  290 us (26%)
  local copies, waits for them, and re-layouts  105 us (9%)
  matrix products  46.7 us (4%)
  starting transfers between devices  27.7 us (2%)
  other arithmetic  15.8 us (1%)
  between operations  15.2 us (1%)
    unnamed x10, waiting for transfers between devices  282 us
    all_gather x1, waiting for transfers between devices, per_device(): lax.all_gather(grad_attended, 'ctx', axis=1, tiled=True)  91.6 us
    reduce_scatter x1, waiting for transfers between devices, per_device(): lax.psum_scatter(jnp.einsum('ufd,ufe->de', hidden_cols, attended, preferr...  90 us
    all_gather x1, blocking collectives, per_device(): panel_rows = lax.all_gather(out_weight, 'dp', axis=1, tiled=True)  77.3 us
    psum x1, blocking collectives, per_device(): kernel_whole = lax.psum(kernel_term.astype(jnp.bfloat16), 'ctx')  68 us
    all_gather x1, waiting for transfers between devices, per_device(): lax.all_gather(value_proj, 'ctx', axis=1, tiled=True)  64.5 us
    all_gather x1, blocking collectives, per_device(): lax.all_gather(conv_weight, 'dp', axis=1, tiled=True).astype(jnp.float32)  64.3 us
    all_gather x1, waiting for transfers between devices, per_device(): weight_full = lax.all_gather(panel_rows, 'ctx', axis=0, tiled=True)  43.9 us
  transfers between devices with their start and end apart: 12, of which 9 were waited for; matrix products, arithmetic and copies ran while one was open for 9% of the time, Pallas kernels for 0%

commit v1 on v0

v1 whole, which is shorter than its diff:
```python
import jax
import jax.numpy as jnp
from jax import lax
from jax.experimental import pallas as pl
from jax.experimental.pallas import tpu as pltpu
from jax.sharding import PartitionSpec as P

BF = jnp.bfloat16
F32 = jnp.float32
N_CTX = 16
N_DP = 32
ROWS = 64
FRAMES = 1024
D = 1536
HD = 768
PAIRS = 6
TARGETS = 2 * PAIRS
TAPS = 31
TILE = 256
CONV_BLOCKS = D // 128
NT = (((1,), (1,)), ((), ()))
TN = (((0,), (0,)), ((), ()))


def target_of(n):
    u, p = n // PAIRS, n % PAIRS
    hi = p // 4
    x = (1 - hi) * p + hi * 2 * (p - 4)
    return 4 * x + 2 * u + hi


def remote(src, dst, send, recv, **axis):
    return pltpu.make_async_remote_copy(
        src_ref=src,
        dst_ref=dst,
        send_sem=send,
        recv_sem=recv,
        device_id=axis,
        device_id_type=pl.DeviceIdType.MESH,
    )


def arrived(dst, sem):
    pltpu.make_async_copy(dst, dst, sem).wait()


def loop(count, body):
    def step(i, carry):
        body(i)
        return carry

    lax.fori_loop(0, count, step, 0)


def mo(value, unit):
    return pl.multiple_of(value, unit)


def kernel(
    len_ref, x_ref, q_ref, k_ref, v_ref, msg_ref, go_ref,
    bo_ref, gi_ref, gq_ref, gk_ref, gv_ref, gw_ref, gt_ref,
    qkv, kx, qm, kt, vt, pt, ds, ot, ob, att_r, att, ga_s, ga_r, dqt, dbuf, grad_r,
    w_a, taps, w_full,
    hid, hb, halo, hp, gcb, ghalo, gp, tgs,
    pp, rs1, rs2s, rs2, own2, rs3s, rs3, own3, ms, mr, th, tr,
    s_p1, r_p1, s_a, r_a, s_w, r_w, s_p2, r_p2, s_h, r_h, s_p3, r_p3, s_p4, r_p4,
    s_rs1, r_rs1, s_rs2, r_rs2, s_rs3, r_rs3, s_dp, r_dp, s_t, r_t,
):
    me = lax.axis_index("ctx")
    dp = lax.axis_index("dp")
    x = me // 4
    yh = (me // 2) % 2
    core = me % 2
    sib = 4 * x + 2 * yh + (1 - core)
    ypart = 4 * x + 2 * (1 - yh) + core
    pair = (1 - core) * x + core * (4 + x // 2)
    works = (core * (x % 2)) == 0
    my_rows = pl.ds(mo(me * ROWS, ROWS), ROWS)
    inputs = (q_ref, k_ref, v_ref)

    barrier = pltpu.get_barrier_semaphore()

    def greet_ctx(i):
        @pl.when(i != me)
        def _():
            pl.semaphore_signal(barrier, inc=1, device_id={"ctx": i}, device_id_type=pl.DeviceIdType.MESH)

    def greet_dp(i):
        @pl.when(i != dp)
        def _():
            pl.semaphore_signal(barrier, inc=1, device_id={"dp": i}, device_id_type=pl.DeviceIdType.MESH)

    loop(N_CTX, greet_ctx)
    loop(N_DP, greet_dp)
    pl.semaphore_wait(barrier, N_CTX + N_DP - 2)

    def p1_parts(a, n):
        src = inputs[a].at[n // PAIRS, :, pl.ds(mo((n % PAIRS) * 128, 128), 128)]
        return src, qkv.at[a, my_rows, :]

    def p1_copy(a, n):
        src, dst = p1_parts(a, n)
        return remote(src, dst, s_p1.at[a * TARGETS + n], r_p1.at[a * N_CTX + me], ctx=target_of(n))

    def p1_start(n):
        t = target_of(n)
        for a in range(3):
            @pl.when(t != me)
            def _():
                p1_copy(a, n).start()

            @pl.when(t == me)
            def _():
                src, dst = p1_parts(a, n)
                pltpu.make_async_copy(src, dst, r_p1.at[a * N_CTX + me]).start()

    loop(TARGETS, p1_start)

    def a_copy(d):
        return remote(msg_ref, w_a.at[dp], s_a.at[d], r_a.at[dp], dp=d)

    def a_start(d):
        @pl.when(d != dp)
        def _():
            a_copy(d).start()

        @pl.when(d == dp)
        def _():
            pltpu.make_async_copy(msg_ref, w_a.at[dp], r_a.at[dp]).start()

    loop(N_DP, a_start)
    tgs[...] = jnp.zeros_like(tgs)
    own3[...] = jnp.zeros_like(own3)
    loop(N_DP, lambda d: arrived(w_a.at[d], r_a.at[d]))
    pieces = w_a[...].astype(F32)
    block = pieces[:, 0:24, :].reshape(HD, 128).T
    taps[...] = pieces.reshape(D, 128).T[96:128, :]

    def w_rows(c):
        return w_full.at[pl.ds(mo(c * 96, 32), 96), :]

    w_full[pl.ds(mo(me * 96, 32), 96), :] = block[0:96, :].astype(BF)

    def w_copy(c, slot, to):
        return remote(w_rows(c), w_rows(c), s_w.at[slot], r_w.at[c], ctx=to)

    def w_y():
        return w_copy(me, 0, ypart)

    def w_x(i, y):
        return w_copy(4 * x + 2 * y + core, 1 + 4 * y + i, 4 * i + 2 * yh + core)

    def w_sib(i):
        return w_copy(2 * i + core, 9 + i, sib)

    w_y().start()

    def w_x_start(y):
        def one(i):
            @pl.when(i != x)
            def _():
                w_x(i, y).start()

        loop(4, one)

    w_x_start(yh)

    lane = lax.broadcasted_iota(jnp.int32, (FRAMES, 128), 1)

    @pl.when(works)
    def _():
        for a in range(3):
            loop(N_CTX, lambda c: arrived(qkv.at[a, pl.ds(mo(c * ROWS, ROWS), ROWS), :], r_p1.at[a * N_CTX + c]))
        row = lax.broadcasted_iota(jnp.int32, (FRAMES, 128), 0)
        bias = jnp.where(row < len_ref[yh], 0.0, -1e30)
        q = qkv[0].astype(F32) * 0.125
        k = qkv[1].astype(F32)
        for h in range(2):
            kx[h] = jnp.where(lane == 64 * (1 - h), bias, k).astype(BF)
            mine = (lane // 64) == h
            qm[h] = jnp.where(mine, q, jnp.where(lane == 64 * (1 - h), 1.0, 0.0)).astype(BF)
        kt[...] = k.T.astype(BF)
        vt[...] = qkv[2].astype(F32).T.astype(BF)

    def forward_head(h):
        @pl.when(works)
        def _():
            def tile(i):
                cols = pl.ds(mo(i * TILE, TILE), TILE)
                s = lax.dot_general(kx[h], qm[h, cols, :], NT, preferred_element_type=F32)
                e = jnp.exp(s - jnp.max(s, axis=0, keepdims=True))
                p = (e * (1.0 / jnp.sum(e, axis=0, keepdims=True))).astype(BF)
                pt[h, :, cols] = p
                ot[64 * h:64 * h + 64, cols] = jnp.dot(
                    vt[64 * h:64 * h + 64, :], p, preferred_element_type=F32
                )

            loop(FRAMES // TILE, tile)

    forward_head(0)
    arrived(w_rows(ypart), r_w.at[ypart])
    w_x_start(1 - yh)
    forward_head(1)

    def p2_copy(c):
        rows = pl.ds(mo(c * ROWS, ROWS), ROWS)
        return remote(ob.at[rows, :], att_r.at[yh, pair], s_p2.at[c], r_p2.at[yh * PAIRS + pair], ctx=c)

    @pl.when(works)
    def _():
        ob[...] = ot[...].T.astype(BF)

        def one(c):
            @pl.when(c != me)
            def _():
                p2_copy(c).start()

            @pl.when(c == me)
            def _():
                pltpu.make_async_copy(
                    ob.at[my_rows, :], att_r.at[yh, pair], r_p2.at[yh * PAIRS + pair]
                ).start()

        loop(N_CTX, one)

    def w_forward(i):
        c = 2 * i + core

        @pl.when(((c - me) * (c - ypart)) != 0)
        def _():
            arrived(w_rows(c), r_w.at[c])

        w_sib(i).start()

    loop(8, w_forward)

    def w_last(i):
        c = 2 * i + (1 - core)
        arrived(w_rows(c), r_w.at[c])

    loop(8, w_last)
    loop(TARGETS, lambda n: arrived(att_r.at[n // PAIRS, n % PAIRS], r_p2.at[n]))
    for u in range(2):
        for p in range(PAIRS):
            att[64 * u:64 * u + 64, 128 * p:128 * p + 128] = att_r[u, p]

    frame = lax.broadcasted_iota(jnp.int32, (ROWS, TILE), 0) + me * ROWS

    def project(i):
        cols = pl.ds(mo(i * TILE, TILE), TILE)
        out = lax.dot_general(att[...], w_full[cols, :], NT, preferred_element_type=F32)
        for u in range(2):
            h = (out[64 * u:64 * u + 64, :] + x_ref[u, :, cols].astype(F32)).astype(BF).astype(F32)
            masked = jnp.where(frame < len_ref[u], h, 0.0)
            hid[u, :, cols] = h
            hb[u, :, cols] = masked.astype(BF)
            hp[u, 16:80, cols] = masked

    loop(D // TILE, project)

    def edges(src, buf, base):
        up = remote(src.at[:, 48:64, :], buf.at[0], s_h.at[base], r_h.at[base], ctx=lax.rem(me + 1, N_CTX))
        down = remote(
            src.at[:, 0:16, :], buf.at[1], s_h.at[base + 1], r_h.at[base + 1], ctx=lax.rem(me + N_CTX - 1, N_CTX)
        )
        return up, down

    def edges_start(src, buf, base):
        up, down = edges(src, buf, base)

        @pl.when(me < N_CTX - 1)
        def _():
            up.start()

        @pl.when(me > 0)
        def _():
            down.start()

    def edges_take(buf, base, padded):
        for side, first in ((0, 0), (1, 80)):
            inner = (me > 0) if side == 0 else (me < N_CTX - 1)

            @pl.when(inner)
            def _():
                arrived(buf.at[side], r_h.at[base + side])
                padded[:, first:first + 16, :] = buf[side].astype(F32)

            @pl.when(jnp.logical_not(inner))
            def _():
                padded[:, first:first + 16, :] = jnp.zeros((2, 16, D), F32)

    def rolled_by(block, r):
        return block if r == 0 else pltpu.roll(block, 96 - r, 0)

    edges_start(hb, halo, 0)
    edges_take(halo, 0, hp)

    def conv_forward(i):
        cols = pl.ds(mo(i * 128, 128), 128)
        w = taps[:, cols]
        for u in range(2):
            block = hp[u, :, cols]
            acc = jnp.zeros((ROWS, 128), F32)
            for r in range(8):
                moved = rolled_by(block, r)
                for a in range(4):
                    j = 8 * a + r - 1
                    if 0 <= j < TAPS:
                        acc = acc + w[j:j + 1, :] * moved[8 * a:8 * a + ROWS, :]
            sg = jax.nn.sigmoid(acc)
            bo_ref[u, :, cols] = (hid[u, :, cols] + acc * sg).astype(BF)
            gc = (go_ref[u, :, cols].astype(F32) * (sg * (1.0 + acc * (1.0 - sg)))).astype(BF)
            gcb[u, :, cols] = gc
            gp[u, 16:80, cols] = gc.astype(F32)

    loop(CONV_BLOCKS, conv_forward)
    edges_start(gcb, ghalo, 2)

    def taps_gradient(i):
        cols = pl.ds(mo(i * 128, 128), 128)
        blocks = [hp[u, :, cols] for u in range(2)]
        grads = [gp[u, 16:80, cols] for u in range(2)]
        for r in range(8):
            moved = [rolled_by(block, r) for block in blocks]
            for a in range(4):
                j = 8 * a + r - 1
                if 0 <= j < TAPS:
                    total = sum(g * m[8 * a:8 * a + ROWS, :] for g, m in zip(grads, moved))
                    tgs[96 + j:97 + j, cols] = jnp.sum(total, axis=0, keepdims=True)

    loop(CONV_BLOCKS, taps_gradient)
    edges_take(ghalo, 2, gp)
    frame_c = lax.broadcasted_iota(jnp.int32, (ROWS, 128), 0) + me * ROWS

    def conv_backward(i):
        cols = pl.ds(mo(i * 128, 128), 128)
        w = taps[:, cols]
        for u in range(2):
            block = gp[u, :, cols]
            acc = jnp.zeros((ROWS, 128), F32)
            for r in range(8):
                moved = rolled_by(block, r)
                for a in range(4):
                    j = 31 - (8 * a + r)
                    if 0 <= j < TAPS:
                        acc = acc + w[j:j + 1, :] * moved[8 * a:8 * a + ROWS, :]
            gi = go_ref[u, :, cols].astype(F32) + jnp.where(frame_c < len_ref[u], acc, 0.0)
            gi_ref[u, :, cols] = gi.astype(BF)

    loop(CONV_BLOCKS, conv_backward)

    def p3_copy(n):
        return remote(
            ga_s.at[n // PAIRS, n % PAIRS], ga_r.at[my_rows, :], s_p3.at[n], r_p3.at[me], ctx=target_of(n)
        )

    gi_rows = gi_ref[...].reshape(2 * ROWS, D)
    for part in range(HD // TILE):
        out = jnp.dot(gi_rows, w_full[:, TILE * part:TILE * part + TILE], preferred_element_type=F32).astype(BF)
        for u in range(2):
            for half in range(2):
                ga_s[u, 2 * part + half] = out[64 * u:64 * u + 64, 128 * half:128 * half + 128]

    def p3_start(n):
        t = target_of(n)

        @pl.when(t != me)
        def _():
            p3_copy(n).start()

        @pl.when(t == me)
        def _():
            pltpu.make_async_copy(ga_s.at[n // PAIRS, n % PAIRS], ga_r.at[my_rows, :], r_p3.at[me]).start()

    loop(TARGETS, p3_start)

    def rs1_copy(i):
        return remote(
            pp.at[pl.ds(2 * i, 2), 1 - core], rs1.at[pl.ds(2 * i, 2)], s_rs1.at[i], r_rs1.at[i], ctx=sib
        )

    def panel(i):
        cols = pl.ds(mo(i * 384, 128), 384)
        gi_cols = jnp.concatenate([gi_ref[0, :, cols], gi_ref[1, :, cols]], axis=0)
        out = lax.dot_general(gi_cols, att[...], TN, preferred_element_type=F32)
        pp[pl.ds(2 * i, 2)] = out.reshape(2, 2, 96, HD).astype(BF)
        rs1_copy(i).start()

    loop(4, panel)

    def rs2_copy(i):
        return remote(rs2s.at[i], rs2.at[x], s_rs2.at[i], r_rs2.at[x], ctx=4 * i + 2 * yh + core)

    def rs2_start(i):
        two = pl.ds(2 * i, 2)
        arrived(rs1.at[two], r_rs1.at[i])
        total = pp[two, core].astype(F32) + rs1[two].astype(F32)

        @pl.when(i != x)
        def _():
            rs2s[i] = total.astype(BF)
            rs2_copy(i).start()

        @pl.when(i == x)
        def _():
            own2[...] = total

    loop(4, rs2_start)

    @pl.when(works)
    def _():
        loop(N_CTX, lambda c: arrived(ga_r.at[pl.ds(mo(c * ROWS, ROWS), ROWS), :], r_p3.at[c]))

    def backward_head(h):
        @pl.when(works)
        def _():
            def tile(i):
                cols = pl.ds(mo(i * TILE, TILE), TILE)
                mine = (lax.broadcasted_iota(jnp.int32, (TILE, 128), 1) // 64) == h
                ga = ga_r[cols, :].astype(F32)
                gm = jnp.where(mine, ga, 0.0)
                prod = gm * ob[cols, :].astype(F32)
                delta = jnp.sum(prod.T, axis=0, keepdims=True)
                gmb = gm.astype(BF)
                dpt = lax.dot_general(qkv[2], gmb, NT, preferred_element_type=F32)
                dst = (pt[h, :, cols].astype(F32) * (dpt - delta)).astype(BF)
                ds[h, :, cols] = dst
                dqt[64 * h:64 * h + 64, cols] = jnp.dot(
                    kt[64 * h:64 * h + 64, :], dst, preferred_element_type=F32
                )

            loop(FRAMES // TILE, tile)

    backward_head(0)

    def rs2_take(i):
        @pl.when(i != x)
        def _():
            arrived(rs2.at[i], r_rs2.at[i])
            own2[...] += rs2[i].astype(F32)

    def rs3_copy():
        return remote(rs3s, rs3, s_rs3, r_rs3, ctx=ypart)

    loop(4, rs2_take)
    rs3s[...] = own2[1 - yh].astype(BF)
    rs3_copy().start()
    backward_head(1)

    def p4_copy(a, c):
        rows = pl.ds(mo(c * ROWS, ROWS), ROWS)
        return remote(
            dbuf.at[a, rows, :], grad_r.at[a, yh, pair], s_p4.at[a * N_CTX + c],
            r_p4.at[a * TARGETS + yh * PAIRS + pair], ctx=c,
        )

    def p4_start(a):
        def one(c):
            @pl.when(c != me)
            def _():
                p4_copy(a, c).start()

            @pl.when(c == me)
            def _():
                pltpu.make_async_copy(
                    dbuf.at[a, my_rows, :], grad_r.at[a, yh, pair], r_p4.at[a * TARGETS + yh * PAIRS + pair]
                ).start()

        loop(N_CTX, one)

    @pl.when(works)
    def _():
        dbuf[0] = (dqt[...].T * 0.125).astype(BF)
        p4_start(0)
        mine = (lane // 64) == 0
        qs = [jnp.where((lane // 64) == h, qkv[0].astype(F32) * 0.125, 0.0).astype(BF) for h in range(2)]
        for h in range(2):
            qm[h] = qs[h]

        def keys(i):
            rows = pl.ds(mo(i * TILE, TILE), TILE)
            out = jnp.dot(ds[0, rows, :], qm[0], preferred_element_type=F32)
            out = out + jnp.dot(ds[1, rows, :], qm[1], preferred_element_type=F32)
            dbuf[1, rows, :] = out.astype(BF)

        loop(FRAMES // TILE, keys)
        p4_start(1)

        def values(i):
            rows = pl.ds(mo(i * TILE, TILE), TILE)
            first = jnp.dot(pt[0, rows, :], ga_r[...], preferred_element_type=F32)
            second = jnp.dot(pt[1, rows, :], ga_r[...], preferred_element_type=F32)
            low = (lax.broadcasted_iota(jnp.int32, (TILE, 128), 1) // 64) == 0
            dbuf[2, rows, :] = jnp.where(low, first, second).astype(BF)

        loop(FRAMES // TILE, values)
        p4_start(2)

    arrived(rs3, r_rs3)
    own3[0:96, :] = own2[yh] + rs3[...].astype(F32)
    columns = own3[...].T.reshape(N_DP, 24, 128)
    tap_rows = tgs[...].T.reshape(N_DP, 48, 128)
    joined = jnp.concatenate([tap_rows[:, 0:24, :] + columns, tap_rows[:, 24:48, :]], axis=1)
    ms[...] = joined.astype(BF)

    def dp_copy(d):
        return remote(ms.at[d], mr.at[dp], s_dp.at[d], r_dp.at[dp], dp=d)

    def dp_start(d):
        @pl.when(d != dp)
        def _():
            dp_copy(d).start()

        @pl.when(d == dp)
        def _():
            pltpu.make_async_copy(ms.at[d], mr.at[dp], r_dp.at[dp]).start()

    loop(N_DP, dp_start)
    loop(N_DP, lambda d: arrived(mr.at[d], r_dp.at[d]))
    total = jnp.sum(mr[...].astype(F32), axis=0)
    gw_ref[...] = total
    th[...] = total.astype(BF)

    def t_copy(c):
        return remote(th, tr.at[me], s_t.at[c], r_t.at[me], ctx=c)

    def t_start(c):
        @pl.when(c != me)
        def _():
            t_copy(c).start()

        @pl.when(c == me)
        def _():
            pltpu.make_async_copy(th, tr.at[me], r_t.at[me]).start()

    loop(N_CTX, t_start)

    def p4_take(a):
        loop(TARGETS, lambda n: arrived(grad_r.at[a, n // PAIRS, n % PAIRS], r_p4.at[a * TARGETS + n]))

    for a, out in ((0, gq_ref), (1, gk_ref), (2, gv_ref)):
        p4_take(a)
        for u in range(2):
            for p in range(PAIRS):
                out[u, :, 128 * p:128 * p + 128] = grad_r[a, u, p]

    loop(N_CTX, lambda c: arrived(tr.at[c], r_t.at[c]))
    gt_ref[...] = jnp.sum(tr[...].astype(F32), axis=0)

    def sent(n):
        @pl.when(target_of(n) != me)
        def _():
            for a in range(3):
                p1_copy(a, n).wait_send()
            p3_copy(n).wait_send()

    loop(TARGETS, sent)

    def sent_dp(d):
        @pl.when(d != dp)
        def _():
            a_copy(d).wait_send()
            dp_copy(d).wait_send()

    loop(N_DP, sent_dp)

    def sent_ctx(c):
        @pl.when(c != me)
        def _():
            t_copy(c).wait_send()

            @pl.when(works)
            def _():
                p2_copy(c).wait_send()
                for a in range(3):
                    p4_copy(a, c).wait_send()

    loop(N_CTX, sent_ctx)
    w_y().wait_send()

    def sent_x(i):
        @pl.when(i != x)
        def _():
            w_x(i, 0).wait_send()
            w_x(i, 1).wait_send()
            rs2_copy(i).wait_send()

        rs1_copy(i).wait_send()

    loop(4, sent_x)
    loop(8, lambda i: w_sib(i).wait_send())
    rs3_copy().wait_send()
    for src, buf, base in ((hb, halo, 0), (gcb, ghalo, 2)):
        up, down = edges(src, buf, base)

        @pl.when(me < N_CTX - 1)
        def _():
            up.wait_send()

        @pl.when(me > 0)
        def _():
            down.wait_send()


def per_device(frame_input, queries, key_proj, value_proj, out_weight, conv_weight, lengths, grad_output):
    left = jnp.pad(out_weight.T, ((0, 24), (0, 0)))
    right = jnp.pad(conv_weight.T, ((0, 0), (0, 1)))
    message = jnp.concatenate([left, right], axis=1)
    vmem = pl.BlockSpec(memory_space=pltpu.VMEM)
    dma = lambda n: pltpu.SemaphoreType.DMA((n,))
    scratch = [
        ((3, FRAMES, 128), BF), ((2, FRAMES, 128), BF), ((2, FRAMES, 128), BF), ((128, FRAMES), BF),
        ((128, FRAMES), BF), ((2, FRAMES, FRAMES), BF), ((2, FRAMES, FRAMES), BF), ((128, FRAMES), F32),
        ((FRAMES, 128), BF), ((2, PAIRS, ROWS, 128), BF), ((2 * ROWS, HD), BF), ((2, PAIRS, ROWS, 128), BF),
        ((FRAMES, 128), BF), ((128, FRAMES), F32), ((3, FRAMES, 128), BF), ((3, 2, PAIRS, ROWS, 128), BF),
        ((N_DP, 48, 128), BF), ((32, D), F32), ((D, HD), BF),
        ((2, ROWS, D), F32), ((2, ROWS, D), BF), ((2, 2, 16, D), BF), ((2, 96, D), F32),
        ((2, ROWS, D), BF), ((2, 2, 16, D), BF), ((2, 96, D), F32), ((128, D), F32),
        ((8, 2, 96, HD), BF), ((8, 96, HD), BF), ((4, 2, 96, HD), BF), ((4, 2, 96, HD), BF),
        ((2, 96, HD), F32), ((96, HD), BF), ((96, HD), BF), ((128, HD), F32),
        ((N_DP, 48, 128), BF), ((N_DP, 48, 128), BF), ((48, 128), BF), ((N_CTX, 48, 128), BF),
    ]
    one = pltpu.SemaphoreType.DMA
    sems = [
        dma(36), dma(48), dma(32), dma(32), dma(17), dma(16), dma(16), dma(12), dma(4), dma(4), dma(12), dma(16),
        dma(48), dma(36), dma(4), dma(4), dma(4), dma(4), one, one, dma(32), dma(32), dma(16), dma(16),
    ]
    shapes = (
        ((2, ROWS, D), BF), ((2, ROWS, D), BF), ((2, ROWS, HD), BF), ((2, ROWS, HD), BF), ((2, ROWS, HD), BF),
        ((48, 128), F32), ((48, 128), F32),
    )
    bo, gi, gq, gk, gv, gw, gt = pl.pallas_call(
        kernel,
        out_shape=[jax.ShapeDtypeStruct(s, t) for s, t in shapes],
        in_specs=[pl.BlockSpec(memory_space=pltpu.SMEM)] + [vmem] * 6,
        out_specs=[vmem] * 7,
        scratch_shapes=[pltpu.VMEM(s, t) for s, t in scratch] + sems,
        compiler_params=pltpu.CompilerParams(
            collective_id=0, has_side_effects=True, vmem_limit_bytes=50 * 1024 * 1024
        ),
        cost_estimate=pl.CostEstimate(flops=3 * 10**9, bytes_accessed=4 * 10**6, transcendentals=2 * 10**6),
    )(lengths, frame_input, queries, key_proj, value_proj, message, grad_output)
    return bo, gi, gq, gk, gv, gw[0:24, 0:96].T, gt[:, 96:96 + TAPS].T


def solution(mesh):
    rows = P("dp", "ctx", None)
    return jax.shard_map(
        per_device,
        mesh=mesh,
        in_specs=(rows, rows, rows, rows, P("ctx", "dp"), P(None, "dp"), P("dp"), rows),
        out_specs=(rows, rows, rows, rows, rows, P("ctx", "dp"), P(None, "dp")),
        check_vma=False,
    )
```

time: 1110 us -> 161 us (0.15)
  waiting for transfers between devices: 605 us -> 0 us
  blocking collectives: 290 us -> 0 us
  Pallas kernels: 0 us -> 147 us
  local copies, waits for them, and re-layouts: 105 us -> 11 us
  matrix products: 46.7 us -> 0 us
  starting transfers between devices: 27.7 us -> 0 us
  other arithmetic: 15.8 us -> 0.08 us
  between operations: 15.2 us -> 0.66 us
    unnamed x10 -> x0, waiting for transfers between devices: 282 us -> none
    all_gather x5 -> x0, waiting for transfers between devices: 231 us -> none  [the longest x1 91.6 us: per_device(): lax.all_gather(grad_attended, 'ctx', axis=1, tiled=True)]
    all_gather x4 -> x0, blocking collectives: 222 us -> none  [the longest x1 77.3 us: per_device(): panel_rows = lax.all_gather(out_weight, 'dp', axis=1, tiled=True)]
    pallas_call x0 -> x1, Pallas kernels: none -> 147 us  [per_device(): pl.pallas_call(kernel, out_shape=[jax.ShapeDtypeStruct(s, t) for s, t in...]
    reduce_scatter x1 -> x0, waiting for transfers between devices: 90 us -> none  [per_device(): lax.psum_scatter(jnp.einsum('ufd,ufe->de', hidden_cols, attended, preferr...]
    psum x1 -> x0, blocking collectives: 68 us -> none  [per_device(): kernel_whole = lax.psum(kernel_term.astype(jnp.bfloat16), 'ctx')]
    dot_general x17 -> x0, matrix products: 37.9 us -> none  [the longest x6 10.3 us: masked_scores(): jnp.einsum('uqgd,ukgd->ugqk', query_block, key_block, preferred_element_t...]
    ppermute x4 -> x0, starting transfers between devices: 27.2 us -> none  [the longest x2 14.1 us: padded_2(): before = lax.ppermute(last, axis, up)]
  transfers between devices with their start and end apart: 12 -> 0, of which waited for: 9 -> 0; matrix products, arithmetic and copies ran while one was open for 9% -> 0% of each run, Pallas kernels for 0% -> 0%
where the time goes in v1:
time: 161 us; the launch traced here: 159 us
  Pallas kernels  147 us (91%)
  local copies, waits for them, and re-layouts  11 us (7%)
    pallas_call x1, Pallas kernels, per_device(): pl.pallas_call(kernel, out_shape=[jax.ShapeDtypeStruct(s, t) for s, t in...  147 us
    unnamed x21, local copies, waits for them, and re-layouts  10.4 us

profile of v1, /device:TPU:1, one launch (start us, length us, event | category | flops | bytes accessed | tf_op | source)
XLA Modules:
  0.0 159.0 jit_solution(6484984909846600795)
XLA Ops:
  0.6 0.0 copy-start.6
  0.6 0.8 copy.15
  1.4 0.0 copy-done.6
  1.4 0.0 copy-start.5
  1.4 0.1 fusion.2.msg_ref
  1.5 0.6 copy-done.5
  2.1 0.0 copy-start
  2.1 1.0 copy-done
  3.1 0.0 copy-start.1
  3.1 1.0 copy-done.1
  4.1 0.0 copy-start.2
  4.1 0.9 copy-done.2
  5.0 0.0 copy-start.3
  5.0 0.9 copy-done.3
  5.9 0.0 copy-start.4
  5.9 0.9 copy-done.4
  6.9 147.3 %shard_map.135 = (bf16[2,64,1536]{2,1,0:T(8,128)(2,1)S(1)}, bf16[2,64,1536]{2,1,0:T(8,128)(2,1)S(1)}, bf16[2,64,768]{2,1,0:T(8,128)(2,1)S(1)}, bf16[2,64,768]{2,...) custom-call(s32[2]{0:T(128)S(1)} %copy-done.5, ...), custom_call_target="tpu_custom_call" | custom-call | flops 3000000000 | bytes 4000000 | tf_op jit(solution)/shard_map/pallas_call | solution.py:632
  154.2 0.6 slice_bitcast_fusion.1
  154.8 0.1 slice_bitcast_fusion
  154.8 0.7 copy.16
  155.5 0.7 copy.22
  156.3 0.7 copy.23
  157.0 0.7 copy.24
  157.7 0.7 copy.25
  158.4 0.7 copy.26
Async XLA Ops:
  0.6 0.8 copy-start.6
  1.4 0.7 copy-start.5
  2.1 1.0 copy-start
  3.1 1.0 copy-start.1
  4.1 0.9 copy-start.2
  5.0 0.9 copy-start.3
  5.9 0.9 copy-start.4

commit v2 on v1

v2 whole, which is shorter than its diff:
```python
import jax
import jax.numpy as jnp
from jax import lax
from jax.experimental import pallas as pl
from jax.experimental.pallas import tpu as pltpu
from jax.sharding import PartitionSpec as P

BF = jnp.bfloat16
F32 = jnp.float32
N_CTX = 16
N_DP = 32
ROWS = 64
FRAMES = 1024
D = 1536
HD = 768
PAIRS = 6
TARGETS = 2 * PAIRS
TAPS = 31
TILE = 256
CONV_BLOCKS = D // 128
NT = (((1,), (1,)), ((), ()))
TN = (((0,), (0,)), ((), ()))


def target_of(n):
    u, p = n // PAIRS, n % PAIRS
    hi = p // 4
    x = (1 - hi) * p + hi * 2 * (p - 4)
    return 4 * x + 2 * u + hi


def remote(src, dst, send, recv, **axis):
    return pltpu.make_async_remote_copy(
        src_ref=src,
        dst_ref=dst,
        send_sem=send,
        recv_sem=recv,
        device_id=axis,
        device_id_type=pl.DeviceIdType.MESH,
    )


def arrived(dst, sem):
    pltpu.make_async_copy(dst, dst, sem).wait()


def loop(count, body):
    def step(i, carry):
        body(i)
        return carry

    lax.fori_loop(0, count, step, 0)


def mo(value, unit):
    return pl.multiple_of(value, unit)


def kernel(
    len_ref, x_ref, q_ref, k_ref, v_ref, msg_ref, go_ref,
    bo_ref, gi_ref, gq_ref, gk_ref, gv_ref, gw_ref, gt_ref,
    x_v, go_v, qkv, kx, qm, kt, vt, pt, ds, ob, att_r, att, ga_s, ga_r, dbuf, grad_r,
    w_a, taps, w_full,
    hid, hb, halo, hp, gcb, ghalo, gp, tgs,
    pp, rs1, rs2s, rs2, own2, rs3s, rs3, own3, ms, mr, tms, tmr, th, tr,
    s_in, s_p1, r_p1, s_a, r_a, s_w, r_w, s_p2, r_p2, s_h, r_h, s_p3, r_p3, s_p4, r_p4,
    s_rs1, r_rs1, s_rs2, r_rs2, s_rs3, r_rs3, s_dp, r_dp, s_td, r_td, s_t, r_t,
):
    me = lax.axis_index("ctx")
    dp = lax.axis_index("dp")
    x = me // 4
    yh = (me // 2) % 2
    core = me % 2
    sib = 4 * x + 2 * yh + (1 - core)
    ypart = 4 * x + 2 * (1 - yh) + core
    pair = (1 - core) * x + core * (4 + x // 2)
    works = (core * (x % 2)) == 0
    my_rows = pl.ds(mo(me * ROWS, ROWS), ROWS)
    inputs = (q_ref, k_ref, v_ref)

    loads = [pltpu.make_async_copy(a, b, s_in.at[i]) for i, (a, b) in enumerate(((x_ref, x_v), (go_ref, go_v)))]
    for load in loads:
        load.start()

    barrier = pltpu.get_barrier_semaphore()

    def greet_ctx(i):
        @pl.when(i != me)
        def _():
            pl.semaphore_signal(barrier, inc=1, device_id={"ctx": i}, device_id_type=pl.DeviceIdType.MESH)

    def greet_dp(i):
        @pl.when(i != dp)
        def _():
            pl.semaphore_signal(barrier, inc=1, device_id={"dp": i}, device_id_type=pl.DeviceIdType.MESH)

    loop(N_CTX, greet_ctx)
    loop(N_DP, greet_dp)
    pl.semaphore_wait(barrier, N_CTX + N_DP - 2)

    def p1_parts(a, n):
        src = inputs[a].at[n // PAIRS, :, pl.ds(mo((n % PAIRS) * 128, 128), 128)]
        return src, qkv.at[a, my_rows, :]

    def p1_copy(a, n):
        src, dst = p1_parts(a, n)
        return remote(src, dst, s_p1.at[a * TARGETS + n], r_p1.at[a * N_CTX + me], ctx=target_of(n))

    def p1_start(a):
        def one(i):
            n = lax.rem(i + me, TARGETS)
            t = target_of(n)

            @pl.when(t != me)
            def _():
                p1_copy(a, n).start()

            @pl.when(t == me)
            def _():
                src, dst = p1_parts(a, n)
                pltpu.make_async_copy(src, dst, r_p1.at[a * N_CTX + me]).start()

        loop(TARGETS, one)

    def a_copy(d):
        return remote(msg_ref, w_a.at[dp], s_a.at[d], r_a.at[dp], dp=d)

    def a_start(i):
        a_copy(lax.rem(i + 1 + dp, N_DP)).start()

    loop(N_DP - 1, a_start)
    pltpu.make_async_copy(msg_ref, w_a.at[dp], r_a.at[dp]).start()
    p1_start(1)
    p1_start(0)
    p1_start(2)
    tgs[...] = jnp.zeros_like(tgs)
    own3[...] = jnp.zeros_like(own3)
    loop(N_DP, lambda d: arrived(w_a.at[d], r_a.at[d]))
    pieces = w_a[...].astype(F32)
    block = pieces[:, 0:24, :].reshape(HD, 128).T
    rest = pieces[:, 24:32, :].reshape(N_DP * 8, 128)
    moved_rest = [pltpu.roll(rest, 96 - 32 * k, 1).reshape(N_DP, 8, 128) for k in range(3)]
    taps[...] = jnp.concatenate([pieces[:, 0:24, :]] + moved_rest, axis=1).reshape(D, 128).T[96:128, :]

    def w_rows(c):
        return w_full.at[pl.ds(mo(c * 96, 32), 96), :]

    w_full[pl.ds(mo(me * 96, 32), 96), :] = block[0:96, :].astype(BF)

    def w_copy(c, slot, to):
        return remote(w_rows(c), w_rows(c), s_w.at[slot], r_w.at[c], ctx=to)

    def w_y():
        return w_copy(me, 0, ypart)

    def w_x(i, y):
        return w_copy(4 * x + 2 * y + core, 1 + 4 * y + i, 4 * i + 2 * yh + core)

    def w_sib(i):
        return w_copy(2 * i + core, 9 + i, sib)

    w_y().start()

    def w_x_start(y):
        def one(i):
            @pl.when(i != x)
            def _():
                w_x(i, y).start()

        loop(4, one)

    w_x_start(yh)

    lane = lax.broadcasted_iota(jnp.int32, (FRAMES, 128), 1)

    def p1_take(a):
        loop(N_CTX, lambda c: arrived(qkv.at[a, pl.ds(mo(c * ROWS, ROWS), ROWS), :], r_p1.at[a * N_CTX + c]))

    @pl.when(works)
    def _():
        p1_take(1)
        row = lax.broadcasted_iota(jnp.int32, (FRAMES, 128), 0)
        bias = jnp.where(row < len_ref[yh], 0.0, -1e30)
        k = qkv[1].astype(F32)
        for h in range(2):
            kx[h] = jnp.where(lane == 64 * (1 - h), bias, k).astype(BF)
        kt[...] = k.T.astype(BF)
        p1_take(0)
        q = qkv[0].astype(F32) * 0.125
        for h in range(2):
            mine = (lane // 64) == h
            qm[h] = jnp.where(mine, q, jnp.where(lane == 64 * (1 - h), 1.0, 0.0)).astype(BF)

    def weights_of(h):
        @pl.when(works)
        def _():
            def tile(i):
                cols = pl.ds(mo(i * TILE, TILE), TILE)
                s = lax.dot_general(kx[h], qm[h, cols, :], NT, preferred_element_type=F32)
                e = jnp.exp(s - jnp.max(s, axis=0, keepdims=True))
                pt[h, :, cols] = (e * (1.0 / jnp.sum(e, axis=0, keepdims=True))).astype(BF)

            loop(FRAMES // TILE, tile)

    weights_of(0)
    arrived(w_rows(ypart), r_w.at[ypart])
    w_x_start(1 - yh)
    weights_of(1)

    def p2_copy(c):
        rows = pl.ds(mo(c * ROWS, ROWS), ROWS)
        return remote(ob.at[rows, :], att_r.at[yh, pair], s_p2.at[c], r_p2.at[yh * PAIRS + pair], ctx=c)

    def p2_start(c):
        @pl.when(c != me)
        def _():
            p2_copy(c).start()

        @pl.when(c == me)
        def _():
            pltpu.make_async_copy(ob.at[my_rows, :], att_r.at[yh, pair], r_p2.at[yh * PAIRS + pair]).start()

    @pl.when(works)
    def _():
        p1_take(2)
        vt[...] = qkv[2].astype(F32).T.astype(BF)

        def tile(i):
            cols = pl.ds(mo(i * TILE, TILE), TILE)
            out = [
                jnp.dot(vt[64 * h:64 * h + 64, :], pt[h, :, cols], preferred_element_type=F32) for h in range(2)
            ]
            ob[cols, :] = jnp.concatenate(out, axis=0).T.astype(BF)
            loop(TILE // ROWS, lambda j: p2_start(i * (TILE // ROWS) + j))

        loop(FRAMES // TILE, tile)

    def w_forward(i):
        c = 2 * i + core

        @pl.when(((c - me) * (c - ypart)) != 0)
        def _():
            arrived(w_rows(c), r_w.at[c])

        w_sib(i).start()

    loop(8, w_forward)

    def w_last(i):
        c = 2 * i + (1 - core)
        arrived(w_rows(c), r_w.at[c])

    loop(8, w_last)
    loop(TARGETS, lambda n: arrived(att_r.at[n // PAIRS, n % PAIRS], r_p2.at[n]))
    for u in range(2):
        for p in range(PAIRS):
            att[64 * u:64 * u + 64, 128 * p:128 * p + 128] = att_r[u, p]

    frame = lax.broadcasted_iota(jnp.int32, (ROWS, TILE), 0) + me * ROWS
    before, after = me > 0, me < N_CTX - 1
    col_tiles = D // TILE

    def edge_copies(src, buf, base, i):
        cols = pl.ds(mo(i * TILE, TILE), TILE)
        up = remote(
            src.at[:, 48:64, cols], buf.at[0, :, :, cols], s_h.at[base + i], r_h.at[base + i],
            ctx=lax.rem(me + 1, N_CTX),
        )
        down = remote(
            src.at[:, 0:16, cols], buf.at[1, :, :, cols], s_h.at[base + 6 + i], r_h.at[base + 6 + i],
            ctx=lax.rem(me + N_CTX - 1, N_CTX),
        )
        return up, down

    def edges_do(src, buf, base, i, what):
        up, down = edge_copies(src, buf, base, i)

        @pl.when(after)
        def _():
            what(up)

        @pl.when(before)
        def _():
            what(down)

    def edges_take(buf, base, padded, i):
        cols = pl.ds(mo(i * TILE, TILE), TILE)
        for side, first, inner in ((0, 0, before), (1, 80, after)):
            @pl.when(inner)
            def _():
                arrived(buf.at[side, :, :, cols], r_h.at[base + 6 * side + i])
                padded[:, first:first + 16, cols] = buf[side, :, :, cols].astype(F32)

            @pl.when(jnp.logical_not(inner))
            def _():
                padded[:, first:first + 16, cols] = jnp.zeros((2, 16, TILE), F32)

    def rolled_by(block, r):
        return block if r == 0 else pltpu.roll(block, 96 - r, 0)

    for load in loads:
        load.wait()

    def project(i):
        cols = pl.ds(mo(i * TILE, TILE), TILE)
        out = lax.dot_general(att[...], w_full[cols, :], NT, preferred_element_type=F32)
        for u in range(2):
            h = (out[64 * u:64 * u + 64, :] + x_v[u, :, cols].astype(F32)).astype(BF).astype(F32)
            masked = jnp.where(frame < len_ref[u], h, 0.0)
            hid[u, :, cols] = h
            hb[u, :, cols] = masked.astype(BF)
            hp[u, 16:80, cols] = masked
        edges_do(hb, halo, 0, i, lambda copy: copy.start())

    loop(col_tiles, project)

    def conv_forward(i):
        edges_take(halo, 0, hp, i)
        for half in range(2):
            cols = pl.ds(mo(i * TILE + half * 128, 128), 128)
            w = taps[:, cols]
            for u in range(2):
                block = hp[u, :, cols]
                acc = jnp.zeros((ROWS, 128), F32)
                for r in range(8):
                    moved = rolled_by(block, r)
                    for a in range(4):
                        j = 8 * a + r - 1
                        if 0 <= j < TAPS:
                            acc = acc + w[j:j + 1, :] * moved[8 * a:8 * a + ROWS, :]
                sg = jax.nn.sigmoid(acc)
                bo_ref[u, :, cols] = (hid[u, :, cols] + acc * sg).astype(BF)
                gc = (go_v[u, :, cols].astype(F32) * (sg * (1.0 + acc * (1.0 - sg)))).astype(BF)
                gcb[u, :, cols] = gc
                gp[u, 16:80, cols] = gc.astype(F32)
        edges_do(gcb, ghalo, 12, i, lambda copy: copy.start())

    loop(col_tiles, conv_forward)

    def taps_gradient(i):
        cols = pl.ds(mo(i * 128, 128), 128)
        blocks = [hp[u, :, cols] for u in range(2)]
        grads = [gp[u, 16:80, cols] for u in range(2)]
        for r in range(8):
            moved = [rolled_by(block, r) for block in blocks]
            for a in range(4):
                j = 8 * a + r - 1
                if 0 <= j < TAPS:
                    total = sum(g * m[8 * a:8 * a + ROWS, :] for g, m in zip(grads, moved))
                    tgs[j:j + 1, cols] = jnp.sum(total, axis=0, keepdims=True)

    loop(CONV_BLOCKS, taps_gradient)
    frame_c = lax.broadcasted_iota(jnp.int32, (ROWS, 128), 0) + me * ROWS

    def conv_backward(i):
        edges_take(ghalo, 12, gp, i)
        for half in range(2):
            cols = pl.ds(mo(i * TILE + half * 128, 128), 128)
            w = taps[:, cols]
            for u in range(2):
                block = gp[u, :, cols]
                acc = jnp.zeros((ROWS, 128), F32)
                for r in range(8):
                    moved = rolled_by(block, r)
                    for a in range(4):
                        j = 31 - (8 * a + r)
                        if 0 <= j < TAPS:
                            acc = acc + w[j:j + 1, :] * moved[8 * a:8 * a + ROWS, :]
                gi = go_v[u, :, cols].astype(F32) + jnp.where(frame_c < len_ref[u], acc, 0.0)
                gi_ref[u, :, cols] = gi.astype(BF)

    loop(col_tiles, conv_backward)

    def p3_copy(n):
        return remote(
            ga_s.at[n // PAIRS, n % PAIRS], ga_r.at[my_rows, :], s_p3.at[n], r_p3.at[me], ctx=target_of(n)
        )

    gi_rows = gi_ref[...].reshape(2 * ROWS, D)

    def p3_start(n):
        t = target_of(n)

        @pl.when(t != me)
        def _():
            p3_copy(n).start()

        @pl.when(t == me)
        def _():
            pltpu.make_async_copy(ga_s.at[n // PAIRS, n % PAIRS], ga_r.at[my_rows, :], r_p3.at[me]).start()

    def cotangent(i):
        cols = pl.ds(mo(i * TILE, TILE), TILE)
        out = jnp.dot(gi_rows, w_full[:, cols], preferred_element_type=F32).astype(BF)
        for u in range(2):
            for half in range(2):
                ga_s[u, 2 * i + half] = out[64 * u:64 * u + 64, 128 * half:128 * half + 128]
        loop(4, lambda m: p3_start((m // 2) * PAIRS + 2 * i + m % 2))

    loop(HD // TILE, cotangent)

    tap_rows = tgs[...].T.reshape(N_DP, 48, 128)
    packed = [tap_rows[:, 0:16, :]] + [
        pltpu.roll(tap_rows[:, 16 * k:16 * k + 16, :].reshape(N_DP * 16, 128), 32 * k, 1).reshape(N_DP, 16, 128)
        for k in (1, 2)
    ]
    tms[...] = (packed[0] + packed[1] + packed[2]).astype(BF)

    def dp_all(src, dst, send, recv):
        def copy(d):
            return remote(src.at[d], dst.at[dp], send.at[d], recv.at[dp], dp=d)

        def start(i):
            copy(lax.rem(i + 1 + dp, N_DP)).start()

        def go():
            loop(N_DP - 1, start)
            pltpu.make_async_copy(src.at[dp], dst.at[dp], recv.at[dp]).start()

        return copy, go

    td_copy, td_start = dp_all(tms, tmr, s_td, r_td)
    dp_copy, dp_start = dp_all(ms, mr, s_dp, r_dp)
    def rs1_copy(i):
        return remote(
            pp.at[pl.ds(2 * i, 2), 1 - core], rs1.at[pl.ds(2 * i, 2)], s_rs1.at[i], r_rs1.at[i], ctx=sib
        )

    def panel(i):
        cols = pl.ds(mo(i * 384, 128), 384)
        gi_cols = jnp.concatenate([gi_ref[0, :, cols], gi_ref[1, :, cols]], axis=0)
        out = lax.dot_general(gi_cols, att[...], TN, preferred_element_type=F32)
        pp[pl.ds(2 * i, 2)] = out.reshape(2, 2, 96, HD).astype(BF)
        rs1_copy(i).start()

    loop(4, panel)
    td_start()

    def rs2_copy(i):
        return remote(rs2s.at[i], rs2.at[x], s_rs2.at[i], r_rs2.at[x], ctx=4 * i + 2 * yh + core)

    def rs2_start(i):
        two = pl.ds(2 * i, 2)
        arrived(rs1.at[two], r_rs1.at[i])
        total = pp[two, core].astype(F32) + rs1[two].astype(F32)

        @pl.when(i != x)
        def _():
            rs2s[i] = total.astype(BF)
            rs2_copy(i).start()

        @pl.when(i == x)
        def _():
            own2[...] = total

    loop(4, rs2_start)

    def p4_copy(a, c):
        rows = pl.ds(mo(c * ROWS, ROWS), ROWS)
        return remote(
            dbuf.at[a, rows, :], grad_r.at[a, yh, pair], s_p4.at[a * N_CTX + c],
            r_p4.at[a * TARGETS + yh * PAIRS + pair], ctx=c,
        )

    def p4_start(a, i):
        def one(j):
            c = i * (TILE // ROWS) + j

            @pl.when(c != me)
            def _():
                p4_copy(a, c).start()

            @pl.when(c == me)
            def _():
                pltpu.make_async_copy(
                    dbuf.at[a, my_rows, :], grad_r.at[a, yh, pair], r_p4.at[a * TARGETS + yh * PAIRS + pair]
                ).start()

        loop(TILE // ROWS, one)

    tile_lane = lax.broadcasted_iota(jnp.int32, (TILE, 128), 1) // 64

    @pl.when(works)
    def _():
        loop(N_CTX, lambda c: arrived(ga_r.at[pl.ds(mo(c * ROWS, ROWS), ROWS), :], r_p3.at[c]))

        def values(i):
            rows = pl.ds(mo(i * TILE, TILE), TILE)
            first = jnp.dot(pt[0, rows, :], ga_r[...], preferred_element_type=F32)
            second = jnp.dot(pt[1, rows, :], ga_r[...], preferred_element_type=F32)
            dbuf[2, rows, :] = jnp.where(tile_lane == 0, first, second).astype(BF)
            p4_start(2, i)

        loop(FRAMES // TILE, values)

    def backward_tile(i):
        cols = pl.ds(mo(i * TILE, TILE), TILE)
        ga = ga_r[cols, :].astype(F32)
        prod = (ga * ob[cols, :].astype(F32)).T
        parts = []
        for h in range(2):
            gmb = jnp.where(tile_lane == h, ga, 0.0).astype(BF)
            delta = jnp.sum(prod[64 * h:64 * h + 64, :], axis=0, keepdims=True)
            dpt = lax.dot_general(qkv[2], gmb, NT, preferred_element_type=F32)
            dst = (pt[h, :, cols].astype(F32) * (dpt - delta)).astype(BF)
            ds[h, :, cols] = dst
            parts.append(jnp.dot(kt[64 * h:64 * h + 64, :], dst, preferred_element_type=F32))
        dbuf[0, cols, :] = (jnp.concatenate(parts, axis=0).T * 0.125).astype(BF)
        p4_start(0, i)

    def backward_half(first):
        @pl.when(works)
        def _():
            loop(2, lambda i: backward_tile(i + first))

    backward_half(0)

    def t_copy(c):
        return remote(th, tr.at[me], s_t.at[c], r_t.at[me], ctx=c)

    def t_start(i):
        t_copy(lax.rem(i + 1 + me, N_CTX)).start()

    loop(N_DP, lambda d: arrived(tmr.at[d], r_td.at[d]))
    th[...] = jnp.sum(tmr[...].astype(F32), axis=0).astype(BF)
    loop(N_CTX - 1, t_start)
    pltpu.make_async_copy(th, tr.at[me], r_t.at[me]).start()

    def rs2_take(i):
        @pl.when(i != x)
        def _():
            arrived(rs2.at[i], r_rs2.at[i])
            own2[...] += rs2[i].astype(F32)

    def rs3_copy():
        return remote(rs3s, rs3, s_rs3, r_rs3, ctx=ypart)

    loop(4, rs2_take)
    rs3s[...] = own2[1 - yh].astype(BF)
    rs3_copy().start()
    backward_half(2)

    @pl.when(works)
    def _():
        for h in range(2):
            qm[h] = jnp.where((lane // 64) == h, qkv[0].astype(F32) * 0.125, 0.0).astype(BF)

        def keys(i):
            rows = pl.ds(mo(i * TILE, TILE), TILE)
            out = jnp.dot(ds[0, rows, :], qm[0], preferred_element_type=F32)
            out = out + jnp.dot(ds[1, rows, :], qm[1], preferred_element_type=F32)
            dbuf[1, rows, :] = out.astype(BF)
            p4_start(1, i)

        loop(FRAMES // TILE, keys)

    arrived(rs3, r_rs3)
    own3[0:96, :] = own2[yh] + rs3[...].astype(F32)
    ms[:, 0:32, :] = jnp.concatenate(
        [own3[...].T.reshape(N_DP, 24, 128), jnp.zeros((N_DP, 8, 128), F32)], axis=1
    ).astype(BF)
    dp_start()

    def p4_take(a):
        loop(TARGETS, lambda n: arrived(grad_r.at[a, n // PAIRS, n % PAIRS], r_p4.at[a * TARGETS + n]))

    for a, out in ((2, gv_ref), (0, gq_ref), (1, gk_ref)):
        p4_take(a)
        for u in range(2):
            for p in range(PAIRS):
                out[u, :, 128 * p:128 * p + 128] = grad_r[a, u, p]

    loop(N_CTX, lambda c: arrived(tr.at[c], r_t.at[c]))
    gt_ref[...] = jnp.sum(tr[...].astype(F32), axis=0)
    loop(N_DP, lambda d: arrived(mr.at[d], r_dp.at[d]))
    gw_ref[...] = jnp.sum(mr[...].astype(F32), axis=0)

    def sent(n):
        @pl.when(target_of(n) != me)
        def _():
            for a in range(3):
                p1_copy(a, n).wait_send()
            p3_copy(n).wait_send()

    loop(TARGETS, sent)

    def sent_dp(d):
        @pl.when(d != dp)
        def _():
            a_copy(d).wait_send()
            dp_copy(d).wait_send()
            td_copy(d).wait_send()

    loop(N_DP, sent_dp)

    def sent_ctx(c):
        @pl.when(c != me)
        def _():
            t_copy(c).wait_send()

            @pl.when(works)
            def _():
                p2_copy(c).wait_send()
                for a in range(3):
                    p4_copy(a, c).wait_send()

    loop(N_CTX, sent_ctx)
    w_y().wait_send()

    def sent_x(i):
        @pl.when(i != x)
        def _():
            w_x(i, 0).wait_send()
            w_x(i, 1).wait_send()
            rs2_copy(i).wait_send()

        rs1_copy(i).wait_send()

    loop(4, sent_x)
    loop(8, lambda i: w_sib(i).wait_send())
    rs3_copy().wait_send()
    for src, buf, base in ((hb, halo, 0), (gcb, ghalo, 12)):
        loop(col_tiles, lambda i: edges_do(src, buf, base, i, lambda copy: copy.wait_send()))


def finish(
    bo, gi, gq, gk, gv, gw_ref, gt_ref, bo_o, gi_o, gq_o, gk_o, gv_o, gw_o, gt_o,
    bo_v, gi_v, gq_v, gk_v, gv_v, gw_v, gt_v, in_sems, out_sems,
):
    held = (bo_v, gi_v, gq_v, gk_v, gv_v, gw_v, gt_v)
    outs = (bo_o, gi_o, gq_o, gk_o, gv_o, gw_o, gt_o)
    loads = [pltpu.make_async_copy(a, b, in_sems.at[i]) for i, (a, b) in enumerate(zip((bo, gi, gq, gk, gv), held))]
    stores = [pltpu.make_async_copy(a, b, out_sems.at[i]) for i, (a, b) in enumerate(zip(held, outs))]
    for load in loads:
        load.start()
    padded = jnp.concatenate([gw_ref[...], jnp.zeros((96, 128), F32)], axis=0).T
    gw_v[...] = padded[0:96, 0:24]
    stores[5].start()
    wide = jnp.concatenate([gt_ref[...], jnp.zeros((112, 128), F32)], axis=0).T
    gt_v[...] = jnp.concatenate([wide[32 * k:32 * k + TAPS, 0:16] for k in range(3)], axis=1)
    stores[6].start()
    for load, store in zip(loads, stores):
        load.wait()
        store.start()
    for store in stores:
        store.wait()


def per_device(frame_input, queries, key_proj, value_proj, out_weight, conv_weight, lengths, grad_output):
    right = jnp.pad(conv_weight.T, ((0, 0), (0, 1)))
    top = jnp.concatenate([out_weight.T, right[0:24]], axis=1)
    low = jnp.concatenate([right[24:32], right[32:40], right[40:48], jnp.zeros((8, 32), BF)], axis=1)
    message = jnp.concatenate([top, low], axis=0)
    vmem = pl.BlockSpec(memory_space=pltpu.VMEM)
    hbm = pl.BlockSpec(memory_space=pltpu.HBM)
    dma = lambda n: pltpu.SemaphoreType.DMA((n,))
    scratch = [
        ((2, ROWS, D), BF), ((2, ROWS, D), BF),
        ((3, FRAMES, 128), BF), ((2, FRAMES, 128), BF), ((2, FRAMES, 128), BF), ((128, FRAMES), BF),
        ((128, FRAMES), BF), ((2, FRAMES, FRAMES), BF), ((2, FRAMES, FRAMES), BF),
        ((FRAMES, 128), BF), ((2, PAIRS, ROWS, 128), BF), ((2 * ROWS, HD), BF), ((2, PAIRS, ROWS, 128), BF),
        ((FRAMES, 128), BF), ((3, FRAMES, 128), BF), ((3, 2, PAIRS, ROWS, 128), BF),
        ((N_DP, 32, 128), BF), ((32, D), F32), ((D, HD), BF),
        ((2, ROWS, D), F32), ((2, ROWS, D), BF), ((2, 2, 16, D), BF), ((2, 96, D), F32),
        ((2, ROWS, D), BF), ((2, 2, 16, D), BF), ((2, 96, D), F32), ((128, D), F32),
        ((8, 2, 96, HD), BF), ((8, 96, HD), BF), ((4, 2, 96, HD), BF), ((4, 2, 96, HD), BF),
        ((2, 96, HD), F32), ((96, HD), BF), ((96, HD), BF), ((128, HD), F32),
        ((N_DP, 32, 128), BF), ((N_DP, 32, 128), BF), ((N_DP, 16, 128), BF), ((N_DP, 16, 128), BF),
        ((16, 128), BF), ((N_CTX, 16, 128), BF),
    ]
    one = pltpu.SemaphoreType.DMA
    sems = [
        dma(2), dma(36), dma(48), dma(32), dma(32), dma(17), dma(16), dma(16), dma(12), dma(24), dma(24), dma(12),
        dma(16), dma(48), dma(36), dma(4), dma(4), dma(4), dma(4), one, one, dma(32), dma(32), dma(32), dma(32),
        dma(16), dma(16),
    ]
    shapes = (
        ((2, ROWS, D), BF), ((2, ROWS, D), BF), ((2, ROWS, HD), BF), ((2, ROWS, HD), BF), ((2, ROWS, HD), BF),
        ((32, 128), F32), ((16, 128), F32),
    )
    bo, gi, gq, gk, gv, gw, gt = pl.pallas_call(
        kernel,
        out_shape=[jax.ShapeDtypeStruct(s, t) for s, t in shapes],
        in_specs=[pl.BlockSpec(memory_space=pltpu.SMEM)] + [hbm] * 4 + [vmem, hbm],
        out_specs=[vmem] * 7,
        scratch_shapes=[pltpu.VMEM(s, t) for s, t in scratch] + sems,
        compiler_params=pltpu.CompilerParams(
            collective_id=0, has_side_effects=True, vmem_limit_bytes=60 * 1024 * 1024
        ),
        cost_estimate=pl.CostEstimate(flops=3 * 10**9, bytes_accessed=4 * 10**6, transcendentals=2 * 10**6),
    )(lengths, frame_input, queries, key_proj, value_proj, message, grad_output)
    final = shapes[0:5] + (((96, 24), F32), ((TAPS, 48), F32))
    return tuple(
        pl.pallas_call(
            finish,
            out_shape=[jax.ShapeDtypeStruct(s, t) for s, t in final],
            in_specs=[hbm] * 5 + [vmem] * 2,
            out_specs=[hbm] * 7,
            scratch_shapes=[pltpu.VMEM(s, t) for s, t in final] + [dma(5), dma(7)],
            compiler_params=pltpu.CompilerParams(vmem_limit_bytes=60 * 1024 * 1024),
            cost_estimate=pl.CostEstimate(flops=10**5, bytes_accessed=3 * 10**6, transcendentals=0),
        )(bo, gi, gq, gk, gv, gw, gt)
    )


def solution(mesh):
    rows = P("dp", "ctx", None)
    return jax.shard_map(
        per_device,
        mesh=mesh,
        in_specs=(rows, rows, rows, rows, P("ctx", "dp"), P(None, "dp"), P("dp"), rows),
        out_specs=(rows, rows, rows, rows, rows, P("ctx", "dp"), P(None, "dp")),
        check_vma=False,
    )
```

time: 161 us -> 135 us (0.84)
  Pallas kernels: 147 us -> 130 us
  local copies, waits for them, and re-layouts: 11 us -> 2.95 us
    pallas_call x1, Pallas kernels: 147 us -> 127 us  [per_device(): pl.pallas_call(kernel, out_shape=[jax.ShapeDtypeStruct(s, t) for s, t in...]
    unnamed x21 -> x3, local copies, waits for them, and re-layouts: 10.4 us -> 1.47 us
    pallas_call x0 -> x1, Pallas kernels: none -> 2.91 us  [per_device(): pl.pallas_call(finish, out_shape=[jax.ShapeDtypeStruct(s, t) for s, t in...]
where the time goes in v2:
time: 135 us; the launch traced here: 134 us
  Pallas kernels  130 us (96%)
  local copies, waits for them, and re-layouts  2.95 us (2%)
    pallas_call x1, Pallas kernels, per_device(): pl.pallas_call(kernel, out_shape=[jax.ShapeDtypeStruct(s, t) for s, t in...  127 us
    pallas_call x1, Pallas kernels, per_device(): pl.pallas_call(finish, out_shape=[jax.ShapeDtypeStruct(s, t) for s, t in...  2.91 us

profile of v2, /device:TPU:1, one launch (start us, length us, event | category | flops | bytes accessed | tf_op | source)
XLA Modules:
  0.0 134.1 jit_solution(5175067206820124812)
XLA Ops:
  0.6 0.8 copy.15
  1.4 0.0 copy-start
  1.5 0.7 copy-done
  2.1 0.7 maximum_maximum_fusion.msg_ref
  2.8 126.9 %shard_map.135 = (bf16[2,64,1536]{2,1,0:T(8,128)(2,1)}, bf16[2,64,1536]{2,1,0:T(8,128)(2,1)}, bf16[2,64,768]{2,1,0:T(8,128)(2,1)}, bf16[2,64,768]{2,1,0:T(8,128)...) custom-call(s32[2]{0:T(128)} %len_ref.1, bf16[2,64,1536]{2,1,0:T(8,128)(2,1)} %x_ref.1, ...), custom_call_target="tpu_custom_call" | custom-call | flops 3000000000 | bytes 4000000 | tf_op jit(solution)/shard_map/pallas_call | solution.py:681
  129.7 2.9 %shard_map.136 = (bf16[2,64,1536]{2,1,0:T(8,128)(2,1)}, bf16[2,64,1536]{2,1,0:T(8,128)(2,1)}, bf16[2,64,768]{2,1,0:T(8,128)(2,1)}, bf16[2,64,768]{2,1,0:T(8,128)...) custom-call(bf16[2,64,1536]{2,1,0:T(8,128)(2,1)} %get-tuple-element.14.bo, ...), custom_call_target="tpu_custom_call" | custom-call | flops 100000 | bytes 3000000 | tf_op jit(solution)/shard_map/pallas_call | solution.py:694
  132.6 1.5 %copy.16 = f32[96,24]{0,1:T(8,128)} copy(f32[96,24]{1,0:T(8,128)} %get-tuple-element.26) | data formatting | bytes 18432 | tf_op jit(solution)/shard_map/pallas_call | solution.py:694
  (3 shorter events, 0.0 us)
Async XLA Ops:
  1.4 0.7 copy-start

commit v3 on v2

--- a/solution.py
+++ b/solution.py
@@ -25,7 +25,7 @@
 def target_of(n):
     u, p = n // PAIRS, n % PAIRS
     hi = p // 4
-    x = (1 - hi) * p + hi * 2 * (p - 4)
+    x = (1 - hi) * p + hi * (2 * (p - 4) + u)
     return 4 * x + 2 * u + hi
 
 
@@ -57,14 +57,14 @@
 
 
 def kernel(
-    len_ref, x_ref, q_ref, k_ref, v_ref, msg_ref, go_ref,
+    len_ref, x_ref, q_ref, k_ref, v_ref, wt_ref, cw_ref, go_ref,
     bo_ref, gi_ref, gq_ref, gk_ref, gv_ref, gw_ref, gt_ref,
     x_v, go_v, qkv, kx, qm, kt, vt, pt, ds, ob, att_r, att, ga_s, ga_r, dbuf, grad_r,
-    w_a, taps, w_full,
+    w_a, taps, w_full, msg_ref,
     hid, hb, halo, hp, gcb, ghalo, gp, tgs,
-    pp, rs1, rs2s, rs2, own2, rs3s, rs3, own3, ms, mr, tms, tmr, th, tr,
-    s_in, s_p1, r_p1, s_a, r_a, s_w, r_w, s_p2, r_p2, s_h, r_h, s_p3, r_p3, s_p4, r_p4,
-    s_rs1, r_rs1, s_rs2, r_rs2, s_rs3, r_rs3, s_dp, r_dp, s_td, r_td, s_t, r_t,
+    pp, rs1, rs2s, rs2, own2, rs3s, rs3, own3, ms, zr, ys, yr, tms, tzr, tys, tyr, th, tr,
+    s_in, s_p1, r_p1, s_ay, r_ay, s_az, r_az, s_w, r_w, s_p2, r_p2, s_h, r_h, s_p3, r_p3, s_p4, r_p4,
+    s_rs1, r_rs1, s_rs2, r_rs2, s_rs3, r_rs3, s_dp, r_dp, s_de, r_de, s_td, r_td, s_te, r_te, s_t, r_t,
 ):
     me = lax.axis_index("ctx")
     dp = lax.axis_index("dp")
@@ -74,7 +74,8 @@
     sib = 4 * x + 2 * yh + (1 - core)
     ypart = 4 * x + 2 * (1 - yh) + core
     pair = (1 - core) * x + core * (4 + x // 2)
-    works = (core * (x % 2)) == 0
+    works = (core * ((x + yh) % 2)) == 0
+    zi, yl = dp // 4, dp % 4
     my_rows = pl.ds(mo(me * ROWS, ROWS), ROWS)
     inputs = (q_ref, k_ref, v_ref)
 
@@ -82,6 +83,12 @@
     for load in loads:
         load.start()
 
+    wide = jnp.concatenate([cw_ref[...].astype(F32), jnp.zeros((TAPS, 80), F32)], axis=1)
+    right = jnp.concatenate([wide, jnp.zeros((128 - TAPS, 128), F32)], axis=0).T[0:48, 0:32]
+    top = jnp.concatenate([wt_ref[...].astype(F32), right[0:24]], axis=1)
+    low = jnp.concatenate([right[24:32], right[32:40], right[40:48], jnp.zeros((8, 32), F32)], axis=1)
+    msg_ref[...] = jnp.concatenate([top, low], axis=0).astype(BF)
+
     barrier = pltpu.get_barrier_semaphore()
 
     def greet_ctx(i):
@@ -89,14 +96,19 @@
         def _():
             pl.semaphore_signal(barrier, inc=1, device_id={"ctx": i}, device_id_type=pl.DeviceIdType.MESH)
 
-    def greet_dp(i):
-        @pl.when(i != dp)
-        def _():
-            pl.semaphore_signal(barrier, inc=1, device_id={"dp": i}, device_id_type=pl.DeviceIdType.MESH)
+    def z_peer(i):
+        return 4 * lax.rem(zi + 1 + i, 8) + yl
+
+    def y_peer(i):
+        return 4 * zi + lax.rem(yl + 1 + i, 4)
+
+    def greet_dp(to):
+        pl.semaphore_signal(barrier, inc=1, device_id={"dp": to}, device_id_type=pl.DeviceIdType.MESH)
 
     loop(N_CTX, greet_ctx)
-    loop(N_DP, greet_dp)
-    pl.semaphore_wait(barrier, N_CTX + N_DP - 2)
+    loop(7, lambda i: greet_dp(z_peer(i)))
+    loop(3, lambda i: greet_dp(y_peer(i)))
+    pl.semaphore_wait(barrier, N_CTX - 1 + 7 + 3)
 
     def p1_parts(a, n):
         src = inputs[a].at[n // PAIRS, :, pl.ds(mo((n % PAIRS) * 128, 128), 128)]
@@ -104,7 +116,7 @@
 
     def p1_copy(a, n):
         src, dst = p1_parts(a, n)
-        return remote(src, dst, s_p1.at[a * TARGETS + n], r_p1.at[a * N_CTX + me], ctx=target_of(n))
+        return remote(src, dst, s_p1, r_p1.at[a], ctx=target_of(n))
 
     def p1_start(a):
         def one(i):
@@ -118,24 +130,32 @@
             @pl.when(t == me)
             def _():
                 src, dst = p1_parts(a, n)
-                pltpu.make_async_copy(src, dst, r_p1.at[a * N_CTX + me]).start()
+                pltpu.make_async_copy(src, dst, r_p1.at[a]).start()
 
         loop(TARGETS, one)
 
-    def a_copy(d):
-        return remote(msg_ref, w_a.at[dp], s_a.at[d], r_a.at[dp], dp=d)
-
-    def a_start(i):
-        a_copy(lax.rem(i + 1 + dp, N_DP)).start()
-
-    loop(N_DP - 1, a_start)
-    pltpu.make_async_copy(msg_ref, w_a.at[dp], r_a.at[dp]).start()
+    four = pl.ds(4 * zi, 4)
+
+    def a_y(i):
+        remote(msg_ref, w_a.at[dp], s_ay, r_ay, dp=y_peer(i)).start()
+
+    def a_z(i):
+        remote(w_a.at[four], w_a.at[four], s_az, r_az.at[zi], dp=z_peer(i)).start()
+
+    def a_z_take(i):
+        source = lax.rem(zi + 1 + i, 8)
+        arrived(w_a.at[pl.ds(4 * source, 4)], r_az.at[source])
+
+    loop(3, a_y)
+    pltpu.make_async_copy(msg_ref, w_a.at[dp], r_ay).start()
     p1_start(1)
+    arrived(w_a.at[four], r_ay)
+    loop(7, a_z)
     p1_start(0)
     p1_start(2)
     tgs[...] = jnp.zeros_like(tgs)
     own3[...] = jnp.zeros_like(own3)
-    loop(N_DP, lambda d: arrived(w_a.at[d], r_a.at[d]))
+    loop(7, a_z_take)
     pieces = w_a[...].astype(F32)
     block = pieces[:, 0:24, :].reshape(HD, 128).T
     rest = pieces[:, 24:32, :].reshape(N_DP * 8, 128)
@@ -174,7 +194,7 @@
     lane = lax.broadcasted_iota(jnp.int32, (FRAMES, 128), 1)
 
     def p1_take(a):
-        loop(N_CTX, lambda c: arrived(qkv.at[a, pl.ds(mo(c * ROWS, ROWS), ROWS), :], r_p1.at[a * N_CTX + c]))
+        arrived(qkv.at[a], r_p1.at[a])
 
     @pl.when(works)
     def _():
@@ -209,7 +229,7 @@
 
     def p2_copy(c):
         rows = pl.ds(mo(c * ROWS, ROWS), ROWS)
-        return remote(ob.at[rows, :], att_r.at[yh, pair], s_p2.at[c], r_p2.at[yh * PAIRS + pair], ctx=c)
+        return remote(ob.at[rows, :], att_r.at[yh, pair], s_p2, r_p2, ctx=c)
 
     def p2_start(c):
         @pl.when(c != me)
@@ -218,7 +238,7 @@
 
         @pl.when(c == me)
         def _():
-            pltpu.make_async_copy(ob.at[my_rows, :], att_r.at[yh, pair], r_p2.at[yh * PAIRS + pair]).start()
+            pltpu.make_async_copy(ob.at[my_rows, :], att_r.at[yh, pair], r_p2).start()
 
     @pl.when(works)
     def _():
@@ -251,7 +271,7 @@
         arrived(w_rows(c), r_w.at[c])
 
     loop(8, w_last)
-    loop(TARGETS, lambda n: arrived(att_r.at[n // PAIRS, n % PAIRS], r_p2.at[n]))
+    arrived(att_r, r_p2)
     for u in range(2):
         for p in range(PAIRS):
             att[64 * u:64 * u + 64, 128 * p:128 * p + 128] = att_r[u, p]
@@ -373,7 +393,7 @@
 
     def p3_copy(n):
         return remote(
-            ga_s.at[n // PAIRS, n % PAIRS], ga_r.at[my_rows, :], s_p3.at[n], r_p3.at[me], ctx=target_of(n)
+            ga_s.at[n // PAIRS, n % PAIRS], ga_r.at[my_rows, :], s_p3, r_p3, ctx=target_of(n)
         )
 
     gi_rows = gi_ref[...].reshape(2 * ROWS, D)
@@ -387,7 +407,7 @@
 
         @pl.when(t == me)
         def _():
-            pltpu.make_async_copy(ga_s.at[n // PAIRS, n % PAIRS], ga_r.at[my_rows, :], r_p3.at[me]).start()
+            pltpu.make_async_copy(ga_s.at[n // PAIRS, n % PAIRS], ga_r.at[my_rows, :], r_p3).start()
 
     def cotangent(i):
         cols = pl.ds(mo(i * TILE, TILE), TILE)
@@ -406,21 +426,38 @@
     ]
     tms[...] = (packed[0] + packed[1] + packed[2]).astype(BF)
 
-    def dp_all(src, dst, send, recv):
-        def copy(d):
-            return remote(src.at[d], dst.at[dp], send.at[d], recv.at[dp], dp=d)
-
-        def start(i):
-            copy(lax.rem(i + 1 + dp, N_DP)).start()
-
-        def go():
-            loop(N_DP - 1, start)
-            pltpu.make_async_copy(src.at[dp], dst.at[dp], recv.at[dp]).start()
-
-        return copy, go
-
-    td_copy, td_start = dp_all(tms, tmr, s_td, r_td)
-    dp_copy, dp_start = dp_all(ms, mr, s_dp, r_dp)
+    def over_dp(src, zr, ys, yr, s_z, r_z, s_y, r_y):
+        def first(i):
+            to = z_peer(i)
+            remote(src.at[pl.ds(to - yl, 4)], zr.at[zi], s_z, r_z, dp=to).start()
+
+        def start():
+            loop(7, first)
+            pltpu.make_async_copy(src.at[four], zr.at[zi], r_z).start()
+
+        def second(i):
+            to = y_peer(i)
+            remote(ys.at[to - 4 * zi], yr.at[yl], s_y, r_y, dp=to).start()
+
+        def turn():
+            arrived(zr, r_z)
+            ys[...] = jnp.sum(zr[...].astype(F32), axis=0).astype(BF)
+            loop(3, second)
+            pltpu.make_async_copy(ys.at[yl], yr.at[yl], r_y).start()
+
+        def end():
+            arrived(yr, r_y)
+            return jnp.sum(yr[...].astype(F32), axis=0)
+
+        def sent():
+            arrived(src.at[0:28], s_z)
+            arrived(ys.at[0:3], s_y)
+
+        return start, turn, end, sent
+
+    td_start, td_turn, td_end, td_sent = over_dp(tms, tzr, tys, tyr, s_td, r_td, s_te, r_te)
+    dp_start, dp_turn, dp_end, dp_sent = over_dp(ms, zr, ys, yr, s_dp, r_dp, s_de, r_de)
+
     def rs1_copy(i):
         return remote(
             pp.at[pl.ds(2 * i, 2), 1 - core], rs1.at[pl.ds(2 * i, 2)], s_rs1.at[i], r_rs1.at[i], ctx=sib
@@ -458,8 +495,7 @@
     def p4_copy(a, c):
         rows = pl.ds(mo(c * ROWS, ROWS), ROWS)
         return remote(
-            dbuf.at[a, rows, :], grad_r.at[a, yh, pair], s_p4.at[a * N_CTX + c],
-            r_p4.at[a * TARGETS + yh * PAIRS + pair], ctx=c,
+            dbuf.at[a, rows, :], grad_r.at[a, yh, pair], s_p4, r_p4.at[a], ctx=c,
         )
 
     def p4_start(a, i):
@@ -472,9 +508,7 @@
 
             @pl.when(c == me)
             def _():
-                pltpu.make_async_copy(
-                    dbuf.at[a, my_rows, :], grad_r.at[a, yh, pair], r_p4.at[a * TARGETS + yh * PAIRS + pair]
-                ).start()
+                pltpu.make_async_copy(dbuf.at[a, my_rows, :], grad_r.at[a, yh, pair], r_p4.at[a]).start()
 
         loop(TILE // ROWS, one)
 
@@ -482,7 +516,7 @@
 
     @pl.when(works)
     def _():
-        loop(N_CTX, lambda c: arrived(ga_r.at[pl.ds(mo(c * ROWS, ROWS), ROWS), :], r_p3.at[c]))
+        arrived(ga_r, r_p3)
 
         def values(i):
             rows = pl.ds(mo(i * TILE, TILE), TILE)
@@ -513,18 +547,7 @@
         def _():
             loop(2, lambda i: backward_tile(i + first))
 
-    backward_half(0)
-
-    def t_copy(c):
-        return remote(th, tr.at[me], s_t.at[c], r_t.at[me], ctx=c)
-
-    def t_start(i):
-        t_copy(lax.rem(i + 1 + me, N_CTX)).start()
-
-    loop(N_DP, lambda d: arrived(tmr.at[d], r_td.at[d]))
-    th[...] = jnp.sum(tmr[...].astype(F32), axis=0).astype(BF)
-    loop(N_CTX - 1, t_start)
-    pltpu.make_async_copy(th, tr.at[me], r_t.at[me]).start()
+    td_turn()
 
     def rs2_take(i):
         @pl.when(i != x)
@@ -538,6 +561,23 @@
     loop(4, rs2_take)
     rs3s[...] = own2[1 - yh].astype(BF)
     rs3_copy().start()
+    backward_half(0)
+
+    def t_copy(c):
+        return remote(th, tr.at[me], s_t, r_t, ctx=c)
+
+    def t_start(i):
+        t_copy(lax.rem(i + 1 + me, N_CTX)).start()
+
+    th[...] = td_end().astype(BF)
+    loop(N_CTX - 1, t_start)
+    pltpu.make_async_copy(th, tr.at[me], r_t).start()
+    arrived(rs3, r_rs3)
+    own3[0:96, :] = own2[yh] + rs3[...].astype(F32)
+    ms[...] = jnp.concatenate(
+        [own3[...].T.reshape(N_DP, 24, 128), jnp.zeros((N_DP, 8, 128), F32)], axis=1
+    ).astype(BF)
+    dp_start()
     backward_half(2)
 
     @pl.when(works)
@@ -554,15 +594,10 @@
 
         loop(FRAMES // TILE, keys)
 
-    arrived(rs3, r_rs3)
-    own3[0:96, :] = own2[yh] + rs3[...].astype(F32)
-    ms[:, 0:32, :] = jnp.concatenate(
-        [own3[...].T.reshape(N_DP, 24, 128), jnp.zeros((N_DP, 8, 128), F32)], axis=1
-    ).astype(BF)
-    dp_start()
+    dp_turn()
 
     def p4_take(a):
-        loop(TARGETS, lambda n: arrived(grad_r.at[a, n // PAIRS, n % PAIRS], r_p4.at[a * TARGETS + n]))
+        arrived(grad_r.at[a], r_p4.at[a])
 
     for a, out in ((2, gv_ref), (0, gq_ref), (1, gk_ref)):
         p4_take(a)
@@ -570,41 +605,29 @@
             for p in range(PAIRS):
                 out[u, :, 128 * p:128 * p + 128] = grad_r[a, u, p]
 
-    loop(N_CTX, lambda c: arrived(tr.at[c], r_t.at[c]))
+    arrived(tr, r_t)
     gt_ref[...] = jnp.sum(tr[...].astype(F32), axis=0)
-    loop(N_DP, lambda d: arrived(mr.at[d], r_dp.at[d]))
-    gw_ref[...] = jnp.sum(mr[...].astype(F32), axis=0)
-
-    def sent(n):
-        @pl.when(target_of(n) != me)
-        def _():
-            for a in range(3):
-                p1_copy(a, n).wait_send()
-            p3_copy(n).wait_send()
-
-    loop(TARGETS, sent)
-
-    def sent_dp(d):
-        @pl.when(d != dp)
-        def _():
-            a_copy(d).wait_send()
-            dp_copy(d).wait_send()
-            td_copy(d).wait_send()
-
-    loop(N_DP, sent_dp)
-
-    def sent_ctx(c):
-        @pl.when(c != me)
-        def _():
-            t_copy(c).wait_send()
-
-            @pl.when(works)
-            def _():
-                p2_copy(c).wait_send()
-                for a in range(3):
-                    p4_copy(a, c).wait_send()
-
-    loop(N_CTX, sent_ctx)
+    gw_ref[...] = dp_end()
+
+    arrived(w_a.at[0:3], s_ay)
+    arrived(w_a.at[0:28], s_az)
+    td_sent()
+    dp_sent()
+    arrived(tr.at[0:N_CTX - 1], s_t)
+    others = ROWS * (N_CTX - 1)
+
+    @pl.when(works)
+    def _():
+        arrived(qkv.at[:, 0:ROWS * (TARGETS - 1), :], s_p1)
+        arrived(ga_r.at[0:ROWS * (TARGETS - 1), :], s_p3)
+        arrived(ob.at[0:others, :], s_p2)
+        arrived(dbuf.at[:, 0:others, :], s_p4)
+
+    @pl.when(jnp.logical_not(works))
+    def _():
+        arrived(qkv.at[:, 0:ROWS * TARGETS, :], s_p1)
+        arrived(ga_r.at[0:ROWS * TARGETS, :], s_p3)
+
     w_y().wait_send()
 
     def sent_x(i):
@@ -633,8 +656,7 @@
     stores = [pltpu.make_async_copy(a, b, out_sems.at[i]) for i, (a, b) in enumerate(zip(held, outs))]
     for load in loads:
         load.start()
-    padded = jnp.concatenate([gw_ref[...], jnp.zeros((96, 128), F32)], axis=0).T
-    gw_v[...] = padded[0:96, 0:24]
+    gw_v[...] = gw_ref[0:24, 0:96]
     stores[5].start()
     wide = jnp.concatenate([gt_ref[...], jnp.zeros((112, 128), F32)], axis=0).T
     gt_v[...] = jnp.concatenate([wide[32 * k:32 * k + TAPS, 0:16] for k in range(3)], axis=1)
@@ -647,10 +669,6 @@
 
 
 def per_device(frame_input, queries, key_proj, value_proj, out_weight, conv_weight, lengths, grad_output):
-    right = jnp.pad(conv_weight.T, ((0, 0), (0, 1)))
-    top = jnp.concatenate([out_weight.T, right[0:24]], axis=1)
-    low = jnp.concatenate([right[24:32], right[32:40], right[40:48], jnp.zeros((8, 32), BF)], axis=1)
-    message = jnp.concatenate([top, low], axis=0)
     vmem = pl.BlockSpec(memory_space=pltpu.VMEM)
     hbm = pl.BlockSpec(memory_space=pltpu.HBM)
     dma = lambda n: pltpu.SemaphoreType.DMA((n,))
@@ -660,19 +678,19 @@
         ((128, FRAMES), BF), ((2, FRAMES, FRAMES), BF), ((2, FRAMES, FRAMES), BF),
         ((FRAMES, 128), BF), ((2, PAIRS, ROWS, 128), BF), ((2 * ROWS, HD), BF), ((2, PAIRS, ROWS, 128), BF),
         ((FRAMES, 128), BF), ((3, FRAMES, 128), BF), ((3, 2, PAIRS, ROWS, 128), BF),
-        ((N_DP, 32, 128), BF), ((32, D), F32), ((D, HD), BF),
+        ((N_DP, 32, 128), BF), ((32, D), F32), ((D, HD), BF), ((32, 128), BF),
         ((2, ROWS, D), F32), ((2, ROWS, D), BF), ((2, 2, 16, D), BF), ((2, 96, D), F32),
         ((2, ROWS, D), BF), ((2, 2, 16, D), BF), ((2, 96, D), F32), ((128, D), F32),
         ((8, 2, 96, HD), BF), ((8, 96, HD), BF), ((4, 2, 96, HD), BF), ((4, 2, 96, HD), BF),
         ((2, 96, HD), F32), ((96, HD), BF), ((96, HD), BF), ((128, HD), F32),
-        ((N_DP, 32, 128), BF), ((N_DP, 32, 128), BF), ((N_DP, 16, 128), BF), ((N_DP, 16, 128), BF),
+        ((N_DP, 32, 128), BF), ((8, 4, 32, 128), BF), ((4, 32, 128), BF), ((4, 32, 128), BF),
+        ((N_DP, 16, 128), BF), ((8, 4, 16, 128), BF), ((4, 16, 128), BF), ((4, 16, 128), BF),
         ((16, 128), BF), ((N_CTX, 16, 128), BF),
     ]
     one = pltpu.SemaphoreType.DMA
     sems = [
-        dma(2), dma(36), dma(48), dma(32), dma(32), dma(17), dma(16), dma(16), dma(12), dma(24), dma(24), dma(12),
-        dma(16), dma(48), dma(36), dma(4), dma(4), dma(4), dma(4), one, one, dma(32), dma(32), dma(32), dma(32),
-        dma(16), dma(16),
+        dma(2), one, dma(3), one, one, one, dma(8), dma(17), dma(16), one, one, dma(24), dma(24), one, one, one,
+        dma(3), dma(4), dma(4), dma(4), dma(4), one, one, one, one, one, one, one, one, one, one, one, one,
     ]
     shapes = (
         ((2, ROWS, D), BF), ((2, ROWS, D), BF), ((2, ROWS, HD), BF), ((2, ROWS, HD), BF), ((2, ROWS, HD), BF),
@@ -681,16 +699,16 @@
     bo, gi, gq, gk, gv, gw, gt = pl.pallas_call(
         kernel,
         out_shape=[jax.ShapeDtypeStruct(s, t) for s, t in shapes],
-        in_specs=[pl.BlockSpec(memory_space=pltpu.SMEM)] + [hbm] * 4 + [vmem, hbm],
+        in_specs=[pl.BlockSpec(memory_space=pltpu.SMEM)] + [hbm] * 4 + [vmem, vmem, hbm],
         out_specs=[vmem] * 7,
         scratch_shapes=[pltpu.VMEM(s, t) for s, t in scratch] + sems,
         compiler_params=pltpu.CompilerParams(
             collective_id=0, has_side_effects=True, vmem_limit_bytes=60 * 1024 * 1024
         ),
         cost_estimate=pl.CostEstimate(flops=3 * 10**9, bytes_accessed=4 * 10**6, transcendentals=2 * 10**6),
-    )(lengths, frame_input, queries, key_proj, value_proj, message, grad_output)
-    final = shapes[0:5] + (((96, 24), F32), ((TAPS, 48), F32))
-    return tuple(
+    )(lengths, frame_input, queries, key_proj, value_proj, out_weight.T, conv_weight, grad_output)
+    final = shapes[0:5] + (((24, 96), F32), ((TAPS, 48), F32))
+    bo, gi, gq, gk, gv, gw, gt = (
         pl.pallas_call(
             finish,
             out_shape=[jax.ShapeDtypeStruct(s, t) for s, t in final],
@@ -701,6 +719,7 @@
             cost_estimate=pl.CostEstimate(flops=10**5, bytes_accessed=3 * 10**6, transcendentals=0),
         )(bo, gi, gq, gk, gv, gw, gt)
     )
+    return bo, gi, gq, gk, gv, gw.T, gt
 
 
 def solution(mesh):

time: 135 us -> 125 us (0.926)
  Pallas kernels: 130 us -> 124 us
  local copies, waits for them, and re-layouts: 2.95 us -> 0 us
    pallas_call x1, Pallas kernels: 127 us -> 121 us  [per_device(): pl.pallas_call(kernel, out_shape=[jax.ShapeDtypeStruct(s, t) for s, t in...]
    pallas_call x1 -> x0, local copies, waits for them, and re-layouts: 1.47 us -> none  [per_device(): pl.pallas_call(finish, out_shape=[jax.ShapeDtypeStruct(s, t) for s, t in...]
    unnamed x3 -> x0, local copies, waits for them, and re-layouts: 1.47 us -> none
where the time goes in v3:
time: 125 us
  Pallas kernels  124 us (99%)
    pallas_call x1, Pallas kernels, per_device(): pl.pallas_call(kernel, out_shape=[jax.ShapeDtypeStruct(s, t) for s, t in...  121 us
    pallas_call x1, Pallas kernels, per_device(): pl.pallas_call(finish, out_shape=[jax.ShapeDtypeStruct(s, t) for s, t in...  2.9 us

profile of v3, /device:TPU:1, one launch (start us, length us, event | category | flops | bytes accessed | tf_op | source)
XLA Modules:
  0.0 124.5 jit_solution(4742100274099590069)
XLA Ops:
  0.6 121.0 %shard_map.135 = (bf16[2,64,1536]{2,1,0:T(8,128)(2,1)}, bf16[2,64,1536]{2,1,0:T(8,128)(2,1)}, bf16[2,64,768]{2,1,0:T(8,128)(2,1)}, bf16[2,64,768]{2,1,0:T(8,128)...) custom-call(s32[2]{0:T(128)} %len_ref.1, bf16[2,64,1536]{2,1,0:T(8,128)(2,1)} %x_ref.1, ...), custom_call_target="tpu_custom_call" | custom-call | flops 3000000000 | bytes 4000000 | tf_op jit(solution)/shard_map/pallas_call | solution.py:699
  121.6 2.9 %shard_map.136 = (bf16[2,64,1536]{2,1,0:T(8,128)(2,1)}, bf16[2,64,1536]{2,1,0:T(8,128)(2,1)}, bf16[2,64,768]{2,1,0:T(8,128)(2,1)}, bf16[2,64,768]{2,1,0:T(8,128)...) custom-call(bf16[2,64,1536]{2,1,0:T(8,128)(2,1)} %get-tuple-element.21.bo, ...), custom_call_target="tpu_custom_call" | custom-call | flops 100000 | bytes 3000000 | tf_op jit(solution)/shard_map/pallas_call | solution.py:712

commit v4 on v3

--- a/solution.py
+++ b/solution.py
@@ -62,9 +62,9 @@
     x_v, go_v, qkv, kx, qm, kt, vt, pt, ds, ob, att_r, att, ga_s, ga_r, dbuf, grad_r,
     w_a, taps, w_full, msg_ref,
     hid, hb, halo, hp, gcb, ghalo, gp, tgs,
-    pp, rs1, rs2s, rs2, own2, rs3s, rs3, own3, ms, zr, ys, yr, tms, tzr, tys, tyr, th, tr,
+    pp, rs1, rs2s, rs2, own2, own3, ms, zr, ys, yr, tms, tzr, tys, tyr, th, tr,
     s_in, s_p1, r_p1, s_ay, r_ay, s_az, r_az, s_w, r_w, s_p2, r_p2, s_h, r_h, s_p3, r_p3, s_p4, r_p4,
-    s_rs1, r_rs1, s_rs2, r_rs2, s_rs3, r_rs3, s_dp, r_dp, s_de, r_de, s_td, r_td, s_te, r_te, s_t, r_t,
+    s_rs1, r_rs1, s_rs2, r_rs2, s_dp, r_dp, s_de, r_de, s_td, r_td, s_te, r_te, s_t, r_t,
 ):
     me = lax.axis_index("ctx")
     dp = lax.axis_index("dp")
@@ -102,13 +102,17 @@
     def y_peer(i):
         return 4 * zi + lax.rem(yl + 1 + i, 4)
 
-    def greet_dp(to):
-        pl.semaphore_signal(barrier, inc=1, device_id={"dp": to}, device_id_type=pl.DeviceIdType.MESH)
+    def ring_peer(i):
+        o = lax.rem(4 * yh + yl + 1 + i, 8)
+        return o // 4, o % 4, {"ctx": 4 * x + 2 * (o // 4) + core, "dp": 4 * zi + o % 4}
+
+    def greet(to):
+        pl.semaphore_signal(barrier, inc=1, device_id=to, device_id_type=pl.DeviceIdType.MESH)
 
     loop(N_CTX, greet_ctx)
-    loop(7, lambda i: greet_dp(z_peer(i)))
-    loop(3, lambda i: greet_dp(y_peer(i)))
-    pl.semaphore_wait(barrier, N_CTX - 1 + 7 + 3)
+    loop(7, lambda i: greet({"dp": z_peer(i)}))
+    loop(7, lambda i: greet(ring_peer(i)[2]))
+    pl.semaphore_wait(barrier, N_CTX - 1 + 7 + 7)
 
     def p1_parts(a, n):
         src = inputs[a].at[n // PAIRS, :, pl.ds(mo((n % PAIRS) * 128, 128), 128)]
@@ -137,49 +141,45 @@
     four = pl.ds(4 * zi, 4)
 
     def a_y(i):
-        remote(msg_ref, w_a.at[dp], s_ay, r_ay, dp=y_peer(i)).start()
+        remote(msg_ref, w_a.at[yh, dp], s_ay, r_ay, **ring_peer(i)[2]).start()
 
     def a_z(i):
-        remote(w_a.at[four], w_a.at[four], s_az, r_az.at[zi], dp=z_peer(i)).start()
+        remote(w_a.at[:, four], w_a.at[:, four], s_az, r_az.at[zi], dp=z_peer(i)).start()
 
     def a_z_take(i):
         source = lax.rem(zi + 1 + i, 8)
-        arrived(w_a.at[pl.ds(4 * source, 4)], r_az.at[source])
-
-    loop(3, a_y)
-    pltpu.make_async_copy(msg_ref, w_a.at[dp], r_ay).start()
+        arrived(w_a.at[:, pl.ds(4 * source, 4)], r_az.at[source])
+
+    loop(7, a_y)
+    pltpu.make_async_copy(msg_ref, w_a.at[yh, dp], r_ay).start()
     p1_start(1)
-    arrived(w_a.at[four], r_ay)
+    arrived(w_a.at[:, four], r_ay)
     loop(7, a_z)
     p1_start(0)
     p1_start(2)
     tgs[...] = jnp.zeros_like(tgs)
     own3[...] = jnp.zeros_like(own3)
     loop(7, a_z_take)
-    pieces = w_a[...].astype(F32)
-    block = pieces[:, 0:24, :].reshape(HD, 128).T
-    rest = pieces[:, 24:32, :].reshape(N_DP * 8, 128)
-    moved_rest = [pltpu.roll(rest, 96 - 32 * k, 1).reshape(N_DP, 8, 128) for k in range(3)]
-    taps[...] = jnp.concatenate([pieces[:, 0:24, :]] + moved_rest, axis=1).reshape(D, 128).T[96:128, :]
+    for y in range(2):
+        pieces = w_a[y].astype(F32)
+        block = pieces[:, 0:24, :].reshape(HD, 128).T
+        w_full[pl.ds(mo((4 * x + 2 * y + core) * 96, 32), 96), :] = block[0:96, :].astype(BF)
+        if y == 0:
+            rest = pieces[:, 24:32, :].reshape(N_DP * 8, 128)
+            moved_rest = [pltpu.roll(rest, 96 - 32 * k, 1).reshape(N_DP, 8, 128) for k in range(3)]
+            taps[...] = jnp.concatenate([pieces[:, 0:24, :]] + moved_rest, axis=1).reshape(D, 128).T[96:128, :]
 
     def w_rows(c):
         return w_full.at[pl.ds(mo(c * 96, 32), 96), :]
 
-    w_full[pl.ds(mo(me * 96, 32), 96), :] = block[0:96, :].astype(BF)
-
     def w_copy(c, slot, to):
         return remote(w_rows(c), w_rows(c), s_w.at[slot], r_w.at[c], ctx=to)
 
-    def w_y():
-        return w_copy(me, 0, ypart)
-
     def w_x(i, y):
         return w_copy(4 * x + 2 * y + core, 1 + 4 * y + i, 4 * i + 2 * yh + core)
 
     def w_sib(i):
         return w_copy(2 * i + core, 9 + i, sib)
-
-    w_y().start()
 
     def w_x_start(y):
         def one(i):
@@ -189,7 +189,8 @@
 
         loop(4, one)
 
-    w_x_start(yh)
+    w_x_start(0)
+    w_x_start(1)
 
     lane = lax.broadcasted_iota(jnp.int32, (FRAMES, 128), 1)
 
@@ -223,8 +224,6 @@
             loop(FRAMES // TILE, tile)
 
     weights_of(0)
-    arrived(w_rows(ypart), r_w.at[ypart])
-    w_x_start(1 - yh)
     weights_of(1)
 
     def p2_copy(c):
@@ -456,7 +455,24 @@
         return start, turn, end, sent
 
     td_start, td_turn, td_end, td_sent = over_dp(tms, tzr, tys, tyr, s_td, r_td, s_te, r_te)
-    dp_start, dp_turn, dp_end, dp_sent = over_dp(ms, zr, ys, yr, s_dp, r_dp, s_de, r_de)
+
+    def dp_first(i):
+        to = z_peer(i)
+        remote(ms.at[:, pl.ds(to - yl, 4)], zr.at[zi], s_dp, r_dp, dp=to).start()
+
+    def dp_start():
+        loop(7, dp_first)
+        pltpu.make_async_copy(ms.at[:, four], zr.at[zi], r_dp).start()
+
+    def dp_second(i):
+        yh_to, yl_to, to = ring_peer(i)
+        remote(ys.at[yh_to, yl_to], yr.at[yh, yl], s_de, r_de, **to).start()
+
+    def dp_turn():
+        arrived(zr, r_dp)
+        ys[...] = jnp.sum(zr[...].astype(F32), axis=0).astype(BF)
+        loop(7, dp_second)
+        pltpu.make_async_copy(ys.at[yh, yl], yr.at[yh, yl], r_de).start()
 
     def rs1_copy(i):
         return remote(
@@ -555,12 +571,13 @@
             arrived(rs2.at[i], r_rs2.at[i])
             own2[...] += rs2[i].astype(F32)
 
-    def rs3_copy():
-        return remote(rs3s, rs3, s_rs3, r_rs3, ctx=ypart)
-
     loop(4, rs2_take)
-    rs3s[...] = own2[1 - yh].astype(BF)
-    rs3_copy().start()
+    for y in range(2):
+        own3[0:96, :] = own2[y]
+        ms[y] = jnp.concatenate(
+            [own3[...].T.reshape(N_DP, 24, 128), jnp.zeros((N_DP, 8, 128), F32)], axis=1
+        ).astype(BF)
+    dp_start()
     backward_half(0)
 
     def t_copy(c):
@@ -572,12 +589,6 @@
     th[...] = td_end().astype(BF)
     loop(N_CTX - 1, t_start)
     pltpu.make_async_copy(th, tr.at[me], r_t).start()
-    arrived(rs3, r_rs3)
-    own3[0:96, :] = own2[yh] + rs3[...].astype(F32)
-    ms[...] = jnp.concatenate(
-        [own3[...].T.reshape(N_DP, 24, 128), jnp.zeros((N_DP, 8, 128), F32)], axis=1
-    ).astype(BF)
-    dp_start()
     backward_half(2)
 
     @pl.when(works)
@@ -607,12 +618,14 @@
 
     arrived(tr, r_t)
     gt_ref[...] = jnp.sum(tr[...].astype(F32), axis=0)
-    gw_ref[...] = dp_end()
-
-    arrived(w_a.at[0:3], s_ay)
-    arrived(w_a.at[0:28], s_az)
+    arrived(yr, r_de)
+    gw_ref[...] = jnp.sum(yr[...].astype(F32).reshape(8, 32, 128), axis=0)
+
+    arrived(w_a.at[0, 0:7], s_ay)
+    arrived(w_a.at[:, 0:28], s_az)
     td_sent()
-    dp_sent()
+    arrived(ms.at[:, 0:28], s_dp)
+    arrived(w_a.at[0, 0:7], s_de)
     arrived(tr.at[0:N_CTX - 1], s_t)
     others = ROWS * (N_CTX - 1)
 
@@ -628,7 +641,6 @@
         arrived(qkv.at[:, 0:ROWS * TARGETS, :], s_p1)
         arrived(ga_r.at[0:ROWS * TARGETS, :], s_p3)
 
-    w_y().wait_send()
 
     def sent_x(i):
         @pl.when(i != x)
@@ -641,7 +653,6 @@
 
     loop(4, sent_x)
     loop(8, lambda i: w_sib(i).wait_send())
-    rs3_copy().wait_send()
     for src, buf, base in ((hb, halo, 0), (gcb, ghalo, 12)):
         loop(col_tiles, lambda i: edges_do(src, buf, base, i, lambda copy: copy.wait_send()))
 
@@ -678,19 +689,19 @@
         ((128, FRAMES), BF), ((2, FRAMES, FRAMES), BF), ((2, FRAMES, FRAMES), BF),
         ((FRAMES, 128), BF), ((2, PAIRS, ROWS, 128), BF), ((2 * ROWS, HD), BF), ((2, PAIRS, ROWS, 128), BF),
         ((FRAMES, 128), BF), ((3, FRAMES, 128), BF), ((3, 2, PAIRS, ROWS, 128), BF),
-        ((N_DP, 32, 128), BF), ((32, D), F32), ((D, HD), BF), ((32, 128), BF),
+        ((2, N_DP, 32, 128), BF), ((32, D), F32), ((D, HD), BF), ((32, 128), BF),
         ((2, ROWS, D), F32), ((2, ROWS, D), BF), ((2, 2, 16, D), BF), ((2, 96, D), F32),
         ((2, ROWS, D), BF), ((2, 2, 16, D), BF), ((2, 96, D), F32), ((128, D), F32),
         ((8, 2, 96, HD), BF), ((8, 96, HD), BF), ((4, 2, 96, HD), BF), ((4, 2, 96, HD), BF),
-        ((2, 96, HD), F32), ((96, HD), BF), ((96, HD), BF), ((128, HD), F32),
-        ((N_DP, 32, 128), BF), ((8, 4, 32, 128), BF), ((4, 32, 128), BF), ((4, 32, 128), BF),
+        ((2, 96, HD), F32), ((128, HD), F32),
+        ((2, N_DP, 32, 128), BF), ((8, 2, 4, 32, 128), BF), ((2, 4, 32, 128), BF), ((2, 4, 32, 128), BF),
         ((N_DP, 16, 128), BF), ((8, 4, 16, 128), BF), ((4, 16, 128), BF), ((4, 16, 128), BF),
         ((16, 128), BF), ((N_CTX, 16, 128), BF),
     ]
     one = pltpu.SemaphoreType.DMA
     sems = [
         dma(2), one, dma(3), one, one, one, dma(8), dma(17), dma(16), one, one, dma(24), dma(24), one, one, one,
-        dma(3), dma(4), dma(4), dma(4), dma(4), one, one, one, one, one, one, one, one, one, one, one, one,
+        dma(3), dma(4), dma(4), dma(4), dma(4), one, one, one, one, one, one, one, one, one, one,
     ]
     shapes = (
         ((2, ROWS, D), BF), ((2, ROWS, D), BF), ((2, ROWS, HD), BF), ((2, ROWS, HD), BF), ((2, ROWS, HD), BF),

time: 125 us -> 113 us (0.904); the launches traced: 125 us -> 111 us
  Pallas kernels: 124 us -> 110 us
    pallas_call x1, Pallas kernels: 121 us -> 107 us  [per_device(): pl.pallas_call(kernel, out_shape=[jax.ShapeDtypeStruct(s, t) for s, t in...]
where the time goes in v4:
time: 113 us; the launch traced here: 111 us
  Pallas kernels  110 us (97%)
    pallas_call x1, Pallas kernels, per_device(): pl.pallas_call(kernel, out_shape=[jax.ShapeDtypeStruct(s, t) for s, t in...  107 us
    pallas_call x1, Pallas kernels, per_device(): pl.pallas_call(finish, out_shape=[jax.ShapeDtypeStruct(s, t) for s, t in...  2.9 us

profile of v4, /device:TPU:1, one launch (start us, length us, event | category | flops | bytes accessed | tf_op | source)
XLA Modules:
  0.0 110.5 jit_solution(1316011439304092108)
XLA Ops:
  0.6 107.0 %shard_map.135 = (bf16[2,64,1536]{2,1,0:T(8,128)(2,1)}, bf16[2,64,1536]{2,1,0:T(8,128)(2,1)}, bf16[2,64,768]{2,1,0:T(8,128)(2,1)}, bf16[2,64,768]{2,1,0:T(8,128)...) custom-call(s32[2]{0:T(128)} %len_ref.1, bf16[2,64,1536]{2,1,0:T(8,128)(2,1)} %x_ref.1, ...), custom_call_target="tpu_custom_call" | custom-call | flops 3000000000 | bytes 4000000 | tf_op jit(solution)/shard_map/pallas_call | solution.py:710
  107.6 2.9 %shard_map.136 = (bf16[2,64,1536]{2,1,0:T(8,128)(2,1)}, bf16[2,64,1536]{2,1,0:T(8,128)(2,1)}, bf16[2,64,768]{2,1,0:T(8,128)(2,1)}, bf16[2,64,768]{2,1,0:T(8,128)...) custom-call(bf16[2,64,1536]{2,1,0:T(8,128)(2,1)} %get-tuple-element.21.bo, ...), custom_call_target="tpu_custom_call" | custom-call | flops 100000 | bytes 3000000 | tf_op jit(solution)/shard_map/pallas_call | solution.py:723

commit v5 on v4

--- a/solution.py
+++ b/solution.py
@@ -122,9 +122,9 @@
         src, dst = p1_parts(a, n)
         return remote(src, dst, s_p1, r_p1.at[a], ctx=target_of(n))
 
-    def p1_start(a):
+    def p1_start(a, u):
         def one(i):
-            n = lax.rem(i + me, TARGETS)
+            n = u * PAIRS + lax.rem(i + me, PAIRS)
             t = target_of(n)
 
             @pl.when(t != me)
@@ -136,7 +136,7 @@
                 src, dst = p1_parts(a, n)
                 pltpu.make_async_copy(src, dst, r_p1.at[a]).start()
 
-        loop(TARGETS, one)
+        loop(PAIRS, one)
 
     four = pl.ds(4 * zi, 4)
 
@@ -152,11 +152,14 @@
 
     loop(7, a_y)
     pltpu.make_async_copy(msg_ref, w_a.at[yh, dp], r_ay).start()
-    p1_start(1)
+    p1_start(1, 1 - yh)
+    p1_start(0, 1 - yh)
     arrived(w_a.at[:, four], r_ay)
     loop(7, a_z)
-    p1_start(0)
-    p1_start(2)
+    p1_start(1, yh)
+    p1_start(0, yh)
+    p1_start(2, 1 - yh)
+    p1_start(2, yh)
     tgs[...] = jnp.zeros_like(tgs)
     own3[...] = jnp.zeros_like(own3)
     loop(7, a_z_take)
@@ -368,7 +371,6 @@
                     total = sum(g * m[8 * a:8 * a + ROWS, :] for g, m in zip(grads, moved))
                     tgs[j:j + 1, cols] = jnp.sum(total, axis=0, keepdims=True)
 
-    loop(CONV_BLOCKS, taps_gradient)
     frame_c = lax.broadcasted_iota(jnp.int32, (ROWS, 128), 0) + me * ROWS
 
     def conv_backward(i):
@@ -418,13 +420,6 @@
 
     loop(HD // TILE, cotangent)
 
-    tap_rows = tgs[...].T.reshape(N_DP, 48, 128)
-    packed = [tap_rows[:, 0:16, :]] + [
-        pltpu.roll(tap_rows[:, 16 * k:16 * k + 16, :].reshape(N_DP * 16, 128), 32 * k, 1).reshape(N_DP, 16, 128)
-        for k in (1, 2)
-    ]
-    tms[...] = (packed[0] + packed[1] + packed[2]).astype(BF)
-
     def over_dp(src, zr, ys, yr, s_z, r_z, s_y, r_y):
         def first(i):
             to = z_peer(i)
@@ -487,7 +482,6 @@
         rs1_copy(i).start()
 
     loop(4, panel)
-    td_start()
 
     def rs2_copy(i):
         return remote(rs2s.at[i], rs2.at[x], s_rs2.at[i], r_rs2.at[x], ctx=4 * i + 2 * yh + core)
@@ -563,7 +557,14 @@
         def _():
             loop(2, lambda i: backward_tile(i + first))
 
-    td_turn()
+    loop(CONV_BLOCKS, taps_gradient)
+    tap_rows = tgs[...].T.reshape(N_DP, 48, 128)
+    packed = [tap_rows[:, 0:16, :]] + [
+        pltpu.roll(tap_rows[:, 16 * k:16 * k + 16, :].reshape(N_DP * 16, 128), 32 * k, 1).reshape(N_DP, 16, 128)
+        for k in (1, 2)
+    ]
+    tms[...] = (packed[0] + packed[1] + packed[2]).astype(BF)
+    td_start()
 
     def rs2_take(i):
         @pl.when(i != x)
@@ -580,15 +581,7 @@
     dp_start()
     backward_half(0)
 
-    def t_copy(c):
-        return remote(th, tr.at[me], s_t, r_t, ctx=c)
-
-    def t_start(i):
-        t_copy(lax.rem(i + 1 + me, N_CTX)).start()
-
-    th[...] = td_end().astype(BF)
-    loop(N_CTX - 1, t_start)
-    pltpu.make_async_copy(th, tr.at[me], r_t).start()
+    td_turn()
     backward_half(2)
 
     @pl.when(works)
@@ -606,6 +599,16 @@
         loop(FRAMES // TILE, keys)
 
     dp_turn()
+
+    def t_copy(c):
+        return remote(th, tr.at[me], s_t, r_t, ctx=c)
+
+    def t_start(i):
+        t_copy(lax.rem(i + 1 + me, N_CTX)).start()
+
+    th[...] = td_end().astype(BF)
+    loop(N_CTX - 1, t_start)
+    pltpu.make_async_copy(th, tr.at[me], r_t).start()
 
     def p4_take(a):
         arrived(grad_r.at[a], r_p4.at[a])

time: 113 us -> 117 us (1.035)
  Pallas kernels: 110 us -> 115 us
    pallas_call x1, Pallas kernels: 107 us -> 112 us  [per_device(): pl.pallas_call(kernel, out_shape=[jax.ShapeDtypeStruct(s, t) for s, t in...]
where the time goes in v5:
time: 117 us; the launch traced here: 115 us
  Pallas kernels  115 us (98%)
    pallas_call x1, Pallas kernels, per_device(): pl.pallas_call(kernel, out_shape=[jax.ShapeDtypeStruct(s, t) for s, t in...  112 us
    pallas_call x1, Pallas kernels, per_device(): pl.pallas_call(finish, out_shape=[jax.ShapeDtypeStruct(s, t) for s, t in...  2.9 us

profile of v5, /device:TPU:1, one launch (start us, length us, event | category | flops | bytes accessed | tf_op | source)
XLA Modules:
  0.0 115.3 jit_solution(12394305139898889965)
XLA Ops:
  0.6 111.8 %shard_map.135 = (bf16[2,64,1536]{2,1,0:T(8,128)(2,1)}, bf16[2,64,1536]{2,1,0:T(8,128)(2,1)}, bf16[2,64,768]{2,1,0:T(8,128)(2,1)}, bf16[2,64,768]{2,1,0:T(8,128)...) custom-call(s32[2]{0:T(128)} %len_ref.1, bf16[2,64,1536]{2,1,0:T(8,128)(2,1)} %x_ref.1, ...), custom_call_target="tpu_custom_call" | custom-call | flops 3000000000 | bytes 4000000 | tf_op jit(solution)/shard_map/pallas_call | solution.py:713
  112.4 2.9 %shard_map.136 = (bf16[2,64,1536]{2,1,0:T(8,128)(2,1)}, bf16[2,64,1536]{2,1,0:T(8,128)(2,1)}, bf16[2,64,768]{2,1,0:T(8,128)(2,1)}, bf16[2,64,768]{2,1,0:T(8,128)...) custom-call(bf16[2,64,1536]{2,1,0:T(8,128)(2,1)} %get-tuple-element.21.bo, ...), custom_call_target="tpu_custom_call" | custom-call | flops 100000 | bytes 3000000 | tf_op jit(solution)/shard_map/pallas_call | solution.py:726

commit v6 on v4

--- a/solution.py
+++ b/solution.py
@@ -368,7 +368,6 @@
                     total = sum(g * m[8 * a:8 * a + ROWS, :] for g, m in zip(grads, moved))
                     tgs[j:j + 1, cols] = jnp.sum(total, axis=0, keepdims=True)
 
-    loop(CONV_BLOCKS, taps_gradient)
     frame_c = lax.broadcasted_iota(jnp.int32, (ROWS, 128), 0) + me * ROWS
 
     def conv_backward(i):
@@ -418,75 +417,75 @@
 
     loop(HD // TILE, cotangent)
 
+    def over_dp(src, zr, ys, yr, s_z, r_z, s_y, r_y):
+        def first(i):
+            to = z_peer(i)
+            remote(src.at[pl.ds(to - yl, 4)], zr.at[zi], s_z, r_z, dp=to).start()
+
+        def start():
+            loop(7, first)
+            pltpu.make_async_copy(src.at[four], zr.at[zi], r_z).start()
+
+        def second(i):
+            to = y_peer(i)
+            remote(ys.at[to - 4 * zi], yr.at[yl], s_y, r_y, dp=to).start()
+
+        def turn():
+            arrived(zr, r_z)
+            ys[...] = jnp.sum(zr[...].astype(F32), axis=0).astype(BF)
+            loop(3, second)
+            pltpu.make_async_copy(ys.at[yl], yr.at[yl], r_y).start()
+
+        def end():
+            arrived(yr, r_y)
+            return jnp.sum(yr[...].astype(F32), axis=0)
+
+        def sent():
+            arrived(src.at[0:28], s_z)
+            arrived(ys.at[0:3], s_y)
+
+        return start, turn, end, sent
+
+    td_start, td_turn, td_end, td_sent = over_dp(tms, tzr, tys, tyr, s_td, r_td, s_te, r_te)
+
+    def dp_first(i):
+        remote(ms.at[:, lax.rem(zi + 1 + i, 8)], zr.at[zi], s_dp, r_dp, dp=z_peer(i)).start()
+
+    def dp_start():
+        loop(7, dp_first)
+        pltpu.make_async_copy(ms.at[:, zi], zr.at[zi], r_dp).start()
+
+    def dp_second(i):
+        yh_to, yl_to, to = ring_peer(i)
+        remote(ys.at[yh_to, yl_to], yr.at[yh, yl], s_de, r_de, **to).start()
+
+    def dp_turn():
+        arrived(zr, r_dp)
+        summed = jnp.sum(zr[...].astype(F32), axis=0).reshape(2, 4, 24, 128)
+        ys[...] = jnp.concatenate([summed, jnp.zeros((2, 4, 8, 128), F32)], axis=2).astype(BF)
+        loop(7, dp_second)
+        pltpu.make_async_copy(ys.at[yh, yl], yr.at[yh, yl], r_de).start()
+
+    def rs1_copy(i):
+        return remote(
+            pp.at[pl.ds(2 * i, 2), 1 - core], rs1.at[pl.ds(2 * i, 2)], s_rs1.at[i], r_rs1.at[i], ctx=sib
+        )
+
+    def panel(i):
+        cols = pl.ds(mo(i * 384, 128), 384)
+        gi_cols = jnp.concatenate([gi_ref[0, :, cols], gi_ref[1, :, cols]], axis=0)
+        out = lax.dot_general(gi_cols, att[...], TN, preferred_element_type=F32)
+        pp[pl.ds(2 * i, 2)] = out.reshape(2, 2, 96, HD).astype(BF)
+        rs1_copy(i).start()
+
+    loop(4, panel)
+    loop(CONV_BLOCKS, taps_gradient)
     tap_rows = tgs[...].T.reshape(N_DP, 48, 128)
     packed = [tap_rows[:, 0:16, :]] + [
         pltpu.roll(tap_rows[:, 16 * k:16 * k + 16, :].reshape(N_DP * 16, 128), 32 * k, 1).reshape(N_DP, 16, 128)
         for k in (1, 2)
     ]
     tms[...] = (packed[0] + packed[1] + packed[2]).astype(BF)
-
-    def over_dp(src, zr, ys, yr, s_z, r_z, s_y, r_y):
-        def first(i):
-            to = z_peer(i)
-            remote(src.at[pl.ds(to - yl, 4)], zr.at[zi], s_z, r_z, dp=to).start()
-
-        def start():
-            loop(7, first)
-            pltpu.make_async_copy(src.at[four], zr.at[zi], r_z).start()
-
-        def second(i):
-            to = y_peer(i)
-            remote(ys.at[to - 4 * zi], yr.at[yl], s_y, r_y, dp=to).start()
-
-        def turn():
-            arrived(zr, r_z)
-            ys[...] = jnp.sum(zr[...].astype(F32), axis=0).astype(BF)
-            loop(3, second)
-            pltpu.make_async_copy(ys.at[yl], yr.at[yl], r_y).start()
-
-        def end():
-            arrived(yr, r_y)
-            return jnp.sum(yr[...].astype(F32), axis=0)
-
-        def sent():
-            arrived(src.at[0:28], s_z)
-            arrived(ys.at[0:3], s_y)
-
-        return start, turn, end, sent
-
-    td_start, td_turn, td_end, td_sent = over_dp(tms, tzr, tys, tyr, s_td, r_td, s_te, r_te)
-
-    def dp_first(i):
-        to = z_peer(i)
-        remote(ms.at[:, pl.ds(to - yl, 4)], zr.at[zi], s_dp, r_dp, dp=to).start()
-
-    def dp_start():
-        loop(7, dp_first)
-        pltpu.make_async_copy(ms.at[:, four], zr.at[zi], r_dp).start()
-
-    def dp_second(i):
-        yh_to, yl_to, to = ring_peer(i)
-        remote(ys.at[yh_to, yl_to], yr.at[yh, yl], s_de, r_de, **to).start()
-
-    def dp_turn():
-        arrived(zr, r_dp)
-        ys[...] = jnp.sum(zr[...].astype(F32), axis=0).astype(BF)
-        loop(7, dp_second)
-        pltpu.make_async_copy(ys.at[yh, yl], yr.at[yh, yl], r_de).start()
-
-    def rs1_copy(i):
-        return remote(
-            pp.at[pl.ds(2 * i, 2), 1 - core], rs1.at[pl.ds(2 * i, 2)], s_rs1.at[i], r_rs1.at[i], ctx=sib
-        )
-
-    def panel(i):
-        cols = pl.ds(mo(i * 384, 128), 384)
-        gi_cols = jnp.concatenate([gi_ref[0, :, cols], gi_ref[1, :, cols]], axis=0)
-        out = lax.dot_general(gi_cols, att[...], TN, preferred_element_type=F32)
-        pp[pl.ds(2 * i, 2)] = out.reshape(2, 2, 96, HD).astype(BF)
-        rs1_copy(i).start()
-
-    loop(4, panel)
     td_start()
 
     def rs2_copy(i):
@@ -574,9 +573,7 @@
     loop(4, rs2_take)
     for y in range(2):
         own3[0:96, :] = own2[y]
-        ms[y] = jnp.concatenate(
-            [own3[...].T.reshape(N_DP, 24, 128), jnp.zeros((N_DP, 8, 128), F32)], axis=1
-        ).astype(BF)
+        ms[y] = own3[...].T.reshape(8, 96, 128).astype(BF)
     dp_start()
     backward_half(0)
 
@@ -624,7 +621,7 @@
     arrived(w_a.at[0, 0:7], s_ay)
     arrived(w_a.at[:, 0:28], s_az)
     td_sent()
-    arrived(ms.at[:, 0:28], s_dp)
+    arrived(zr.at[0:7], s_dp)
     arrived(w_a.at[0, 0:7], s_de)
     arrived(tr.at[0:N_CTX - 1], s_t)
     others = ROWS * (N_CTX - 1)
@@ -694,7 +691,7 @@
         ((2, ROWS, D), BF), ((2, 2, 16, D), BF), ((2, 96, D), F32), ((128, D), F32),
         ((8, 2, 96, HD), BF), ((8, 96, HD), BF), ((4, 2, 96, HD), BF), ((4, 2, 96, HD), BF),
         ((2, 96, HD), F32), ((128, HD), F32),
-        ((2, N_DP, 32, 128), BF), ((8, 2, 4, 32, 128), BF), ((2, 4, 32, 128), BF), ((2, 4, 32, 128), BF),
+        ((2, 8, 96, 128), BF), ((8, 2, 96, 128), BF), ((2, 4, 32, 128), BF), ((2, 4, 32, 128), BF),
         ((N_DP, 16, 128), BF), ((8, 4, 16, 128), BF), ((4, 16, 128), BF), ((4, 16, 128), BF),
         ((16, 128), BF), ((N_CTX, 16, 128), BF),
     ]

time: 113 us -> 114 us (level)
    pallas_call x1, Pallas kernels: 107 us -> 108 us  [per_device(): pl.pallas_call(kernel, out_shape=[jax.ShapeDtypeStruct(s, t) for s, t in...]
where the time goes in v6:
time: 114 us; the launch traced here: 112 us
  Pallas kernels  111 us (97%)
    pallas_call x1, Pallas kernels, per_device(): pl.pallas_call(kernel, out_shape=[jax.ShapeDtypeStruct(s, t) for s, t in...  108 us
    pallas_call x1, Pallas kernels, per_device(): pl.pallas_call(finish, out_shape=[jax.ShapeDtypeStruct(s, t) for s, t in...  2.9 us

profile of v6, /device:TPU:1, one launch (start us, length us, event | category | flops | bytes accessed | tf_op | source)
XLA Modules:
  0.0 111.9 jit_solution(13302195033605982426)
XLA Ops:
  0.6 108.4 %shard_map.135 = (bf16[2,64,1536]{2,1,0:T(8,128)(2,1)}, bf16[2,64,1536]{2,1,0:T(8,128)(2,1)}, bf16[2,64,768]{2,1,0:T(8,128)(2,1)}, bf16[2,64,768]{2,1,0:T(8,128)...) custom-call(s32[2]{0:T(128)} %len_ref.1, bf16[2,64,1536]{2,1,0:T(8,128)(2,1)} %x_ref.1, ...), custom_call_target="tpu_custom_call" | custom-call | flops 3000000000 | bytes 4000000 | tf_op jit(solution)/shard_map/pallas_call | solution.py:707
  109.0 2.9 %shard_map.136 = (bf16[2,64,1536]{2,1,0:T(8,128)(2,1)}, bf16[2,64,1536]{2,1,0:T(8,128)(2,1)}, bf16[2,64,768]{2,1,0:T(8,128)(2,1)}, bf16[2,64,768]{2,1,0:T(8,128)...) custom-call(bf16[2,64,1536]{2,1,0:T(8,128)(2,1)} %get-tuple-element.21.bo, ...), custom_call_target="tpu_custom_call" | custom-call | flops 100000 | bytes 3000000 | tf_op jit(solution)/shard_map/pallas_call | solution.py:720
